TPU v7x, 512 devices: a whole 4x8x8 slice. The times are simulated.
512 devices in a mesh: tm: 16 (over y, core), chan: 32 (over z, x).
Axes of the slice: x: 4, y: 8, z: 8, core: 2. Of those that a mesh axis runs over, the one named last changes fastest.
Arguments:
- records: bfloat16 [768, 16384], P('chan', 'tm'), may hold values from -40 to 40
- template_waves: bfloat16 [256, 12, 256], P('chan', None, 'tm'), may hold values from -11 to 11
- channel_lists: int32 [256, 12], replicated, may hold values from -1 to 767, as said below
- moveouts: int32 [256, 12], replicated, may hold values from 0 to 191
- owner_map: int32 [256, 1], replicated, may hold values from 0 to 31; in each aligned block of 8 rows (0 to 7, 8 to 15, ...) at most 2 rows name the same one
Outputs:
- stacks: float32 [2048, 16384], P('chan', 'tm')
Inputs may be any that keep to these rules, and one draw needn't show every extreme that they name: `channel_lists`: template k lists n of 8 to 12 channels in slots 0 to n - 1, slot j holding (3 k + r + j) mod 768 with an offset r of 0 to 5 of its own; later slots are -1. Some template has r = 5 and n = 12. `owner_map`: among the templates of one block of 8 (equal k // 8) no owner is named more than 2 times.
All inputs are finite; a program needn't handle non-finite values.
Results may differ from a plain program's by a relative error of at most 0.0003.
Values may be sent and summed in bfloat16 or wider, within the bound.
No kernel may reach another device: no remote copies, remote signals or barrier semaphores. Data moves between devices by JAX's collectives and lax.ppermute only.
A program may use at most 64 MiB of HBM per device.

v0:
```python
import jax
import jax.numpy as jnp
from jax import lax
from jax.sharding import PartitionSpec as P

L = 256
SLOTS = 12
MAXMV = 192
SPILL = 16
BLOCK = 128


def passed_along(value, axis, steps):
    count = lax.axis_size(axis)
    pairs = [(source, (source + steps) % count) for source in range(count)]
    return lax.ppermute(value, axis, pairs)


def window_energy(squares, length_out, tap_count):
    block_len = 32
    blocks_n = length_out // block_len
    full_blocks = tap_count // block_len
    needed = (blocks_n + full_blocks + 1) * block_len
    squares = jnp.pad(squares, ((0, 0), (0, needed - squares.shape[1])))
    row_count = squares.shape[0]
    blocks = squares.reshape(row_count, blocks_n + full_blocks + 1, block_len)
    inner_sum = jnp.cumsum(blocks, axis=2)
    before = inner_sum - blocks
    totals = inner_sum[:, :, block_len - 1 :]
    energy = totals[:, :blocks_n] - before[:, :blocks_n]
    for offset in range(1, full_blocks):
        energy = energy + totals[:, offset : offset + blocks_n]
    energy = energy + before[:, full_blocks : full_blocks + blocks_n]
    return energy.reshape(row_count, blocks_n * block_len)


def local(records, template_waves, channel_lists, moveouts, owner_map):
    ch_dev, t_dev = records.shape
    n_chan = lax.axis_size("chan")
    tpl_dev = ch_dev // 3
    total_chan = ch_dev * n_chan
    slot_cap = max(2, 2 * tpl_dev // n_chan)
    reach = L + MAXMV
    next_rows = passed_along(records[:SPILL], "chan", -1)
    joined_rows = jnp.concatenate([records, next_rows], axis=0)
    later = passed_along(joined_rows[:, :reach], "tm", -1)
    extended = jnp.concatenate([joined_rows, later], axis=1)
    full_waves = lax.all_gather(template_waves, "tm", axis=2, tiled=True)
    as_float = extended.astype(jnp.float32)
    energy = window_energy(as_float * as_float, t_dev + MAXMV, L)
    frame_width = BLOCK + L
    pieces_n = frame_width // BLOCK
    wide_blocks = (t_dev + MAXMV + BLOCK - 1) // BLOCK
    wide_len = wide_blocks * BLOCK
    row_total = extended.shape[0]
    padded_rows = jnp.pad(extended, ((0, 0), (0, wide_len + L - extended.shape[1])))
    frames = jnp.concatenate(
        [
            padded_rows[:, k_idx * BLOCK : k_idx * BLOCK + wide_len].reshape(
                row_total, wide_blocks, BLOCK
            )
            for k_idx in range(pieces_n)
        ],
        axis=2,
    )
    block_id = lax.axis_index("chan")
    first_tpl = block_id * tpl_dev
    my_lists = lax.dynamic_slice_in_dim(channel_lists, first_tpl, tpl_dev, 0)
    my_shifts = lax.dynamic_slice_in_dim(moveouts, first_tpl, tpl_dev, 0)
    my_owner = lax.dynamic_slice_in_dim(owner_map, first_tpl, tpl_dev, 0)[:, 0]
    is_valid = my_lists >= 0
    local_row = jnp.where(is_valid, jnp.mod(my_lists - block_id * ch_dev, total_chan), 0)
    group_size = max(1, tpl_dev // 16)
    n_groups = tpl_dev // group_size

    def window_at(row_e, shift_e):
        return lax.dynamic_slice_in_dim(row_e, shift_e, t_dev)

    def one_template(rows_t, shifts_t, waves_t, valid_t):
        framed = frames[rows_t]
        padded_wave = jnp.concatenate(
            [waves_t, jnp.zeros((SLOTS, frame_width + 1 - L), waves_t.dtype)], axis=1
        )
        banded = jnp.tile(padded_wave, (1, BLOCK))[:, : BLOCK * frame_width].reshape(
            SLOTS, BLOCK, frame_width
        )
        unshifted = jnp.einsum(
            "suv,sbv->sbu", banded, framed, preferred_element_type=jnp.float32
        ).reshape(SLOTS, wide_len)
        corr = jax.vmap(window_at)(unshifted, shifts_t)
        window = jax.vmap(window_at)(energy[rows_t], shifts_t)
        wave_f = waves_t.astype(jnp.float32)
        wave_sq = jnp.sum(wave_f * wave_f, axis=1)
        normed = corr / jnp.sqrt(wave_sq[:, None] * window + 1e-06)
        normed = jnp.where(valid_t[:, None], normed, jnp.zeros_like(normed))
        return jnp.sum(normed, axis=0)

    def per_group(operands):
        rows_g, shifts_g, waves_g, valid_g = operands
        return jax.vmap(one_template)(rows_g, shifts_g, waves_g, valid_g)

    grouped = (
        local_row.reshape(n_groups, group_size, SLOTS),
        my_shifts.reshape(n_groups, group_size, SLOTS),
        full_waves.reshape(n_groups, group_size, SLOTS, L),
        is_valid.reshape(n_groups, group_size, SLOTS),
    )
    detect = lax.map(per_group, grouped).reshape(tpl_dev, t_dev)
    tpl_ids = jnp.arange(tpl_dev, dtype=jnp.int32)
    same_owner = (my_owner[:, None] == my_owner[None, :]) & (tpl_ids[None, :] < tpl_ids[:, None])
    slot_rank = jnp.sum(same_owner.astype(jnp.int32), axis=1)
    target = my_owner * slot_cap + slot_rank
    outgoing = (
        jnp.zeros((n_chan * slot_cap, t_dev), jnp.float32)
        .at[target]
        .set(detect)
        .reshape(n_chan, slot_cap, t_dev)
    )
    incoming = lax.all_to_all(outgoing, "chan", split_axis=0, concat_axis=0, tiled=True)
    return incoming.reshape(n_chan * slot_cap, t_dev)


def solution(mesh):
    in_specs = (P("chan", "tm"), P("chan", None, "tm"), P(), P(), P())
    out_specs = P("chan", "tm")
    return jax.shard_map(local, mesh=mesh, in_specs=in_specs, out_specs=out_specs, check_vma=False)
```

profile of v0, /device:TPU:1, one launch (start us, length us, event | category | flops | bytes accessed | tf_op | source)
XLA Modules:
  0.0 505.6 jit_solution(2796656859502263374)
XLA Ops:
  0.8 13.7 %collective-permute-start = (bf16[16,1024]{1,0:T(8,128)(2,1)S(1)}, bf16[16,1024]{1,0:T(8,128)(2,1)S(1)}, u32[]{:S(2)}, u32[]{:S(2)}) collective-permute-start(bf16[16,1024]{1,0:T(8,128)(2,1)S(1)} %slice.59), channel_id=1, source_target_pairs={{0,31},{1,0},{2,1},{3,2},{4,3},{5,4},{6,5},{7,6},{8,7},{9,8},{10,9... | collective-permute-start | bytes 98312 | tf_op jit(solution)/shard_map/ppermute | solution.py:16
  18.1 1.3 fusion.27
  20.3 19.4 %all_gather.3 = bf16[8,12,256]{1,0,2:T(8,128)(2,1)S(1)} all-gather(bf16[8,12,16]{1,0,2:T(8,128)(2,1)S(1)} %copy.26), channel_id=1, replica_groups=mesh['tm'=16,'chan'=32] {'tm'}, dimensions={2}, use_global_device_ids=true | all-gather | bytes 52224 | tf_op jit(solution)/shard_map/all_gather | solution.py:48
  40.4 7.9 %reduce_window_sum.11 = f32[40,47,32]{2,1,0:T(8,128)S(1)} reduce-window(f32[40,47,32]{2,1,0:T(8,128)S(1)} %reshape.273, f32[]{:T(128)} %constant.29.clone.1), window={size=1x1x32 pad=0_0x0_0x31_0}, to_apply=%region_1.2 | reduce-window | flops 1864960 | bytes 481284 | tf_op jit(solution)/shard_map/jit(cumsum)/reduce_window_sum | solution.py:27
  48.4 3.5 slice_reduce_fusion.7
  51.8 2.1 slice_add_fusion
  55.3 431.3 %while.16 = (s32[]{:T(128)}, f32[8,1,1024]{2,0,1:T(8,128)S(1)}, pred[8,1,12]{2,0,1:T(8,128)(4,1)S(1)}, s32[8,1,12]{2,1,0:T(1,128)S(1)}, bf16[40,10,384]{2,1,0:T(...) while((s32[]{:T(128)}, f32[8,1,1024]{2,0,1:T(8,128)S(1)}, ...), condition=%wide.region_5.6_spmd, body=%wide.region_2.5_spmd.sunk | while | flops 11867334 | bytes 11543235 | solution.py:108
  55.3 1.6 gather_fusion.1
  57.2 2.3 tile.14
  60.5 23.9 %while.18 = (s32[]{:T(128)}, f32[1,12,1280]{2,1,0:T(8,128)S(1)}, s32[12,3]{0,1:T(4,128)S(1)}, f32[12,1024]{1,0:T(8,128)S(1)}, s32[]{:T(128)}, /*index=5*/s32[]{:T(128)}) while((s32[]{:T(128)}, f32[1,12,1280]{2,1,0:T(8,128)S(1)}, s32[12,3]{0,1:T(4,128)S(1)}, f32[12,1024]{1,0:T(8,128)S(1)}, s32[]{:T(128)}, /*index=5*/s32[]{:T(128)}) %tuple.79), condition=%wide.while_cond, body=%wide.while_body.sunk | while | flops 2 | bytes 16509 | solution.py:77
  61.1 1.3 dynamic-slice_bitcast_fusion.10
  63.1 1.3 dynamic-slice_bitcast_fusion.10
  65.1 1.3 dynamic-slice_bitcast_fusion.10
  67.1 1.3 dynamic-slice_bitcast_fusion.10
  69.1 1.3 dynamic-slice_bitcast_fusion.10
  71.1 1.3 dynamic-slice_bitcast_fusion.10
  73.1 1.3 dynamic-slice_bitcast_fusion.10
  75.1 1.3 dynamic-slice_bitcast_fusion.10
  77.1 1.3 dynamic-slice_bitcast_fusion.10
  79.1 1.3 dynamic-slice_bitcast_fusion.10
  81.1 1.3 dynamic-slice_bitcast_fusion.10
  83.1 1.3 dynamic-slice_bitcast_fusion.10
  85.0 23.9 %while.17 = (s32[]{:T(128)}, f32[1,12,1216]{2,1,0:T(8,128)S(1)}, s32[12,3]{0,1:T(4,128)S(1)}, f32[12,1024]{1,0:T(8,128)S(1)}, s32[]{:T(128)}, /*index=5*/s32[]{:T(128)}) while((s32[]{:T(128)}, f32[1,12,1216]{2,1,0:T(8,128)S(1)}, s32[12,3]{0,1:T(4,128)S(1)}, f32[12,1024]{1,0:T(8,128)S(1)}, s32[]{:T(128)}, /*index=5*/s32[]{:T(128)}) %tuple.85), condition=%wide.while_cond.1, body=%wide.while_body.1.sunk | while | flops 2 | bytes 16509 | solution.py:77
  85.7 1.3 dynamic-slice_bitcast_fusion.9
  87.7 1.3 dynamic-slice_bitcast_fusion.9
  89.7 1.3 dynamic-slice_bitcast_fusion.9
  109.3 1.6 gather_fusion.1
  111.1 2.3 tile.14
  114.4 23.9 %while.18 = (s32[]{:T(128)}, f32[1,12,1280]{2,1,0:T(8,128)S(1)}, s32[12,3]{0,1:T(4,128)S(1)}, f32[12,1024]{1,0:T(8,128)S(1)}, s32[]{:T(128)}, /*index=5*/s32[]{:T(128)}) while((s32[]{:T(128)}, f32[1,12,1280]{2,1,0:T(8,128)S(1)}, s32[12,3]{0,1:T(4,128)S(1)}, f32[12,1024]{1,0:T(8,128)S(1)}, s32[]{:T(128)}, /*index=5*/s32[]{:T(128)}) %tuple.79), condition=%wide.while_cond, body=%wide.while_body.sunk | while | flops 2 | bytes 16509 | solution.py:77
  138.9 23.9 %while.17 = (s32[]{:T(128)}, f32[1,12,1216]{2,1,0:T(8,128)S(1)}, s32[12,3]{0,1:T(4,128)S(1)}, f32[12,1024]{1,0:T(8,128)S(1)}, s32[]{:T(128)}, /*index=5*/s32[]{:T(128)}) while((s32[]{:T(128)}, f32[1,12,1216]{2,1,0:T(8,128)S(1)}, s32[12,3]{0,1:T(4,128)S(1)}, f32[12,1024]{1,0:T(8,128)S(1)}, s32[]{:T(128)}, /*index=5*/s32[]{:T(128)}) %tuple.85), condition=%wide.while_cond.1, body=%wide.while_body.1.sunk | while | flops 2 | bytes 16509 | solution.py:77
  151.5 1.3 dynamic-slice_bitcast_fusion.9
  163.2 1.6 gather_fusion.1
  165.1 2.3 tile.14
  168.3 23.9 %while.18 = (s32[]{:T(128)}, f32[1,12,1280]{2,1,0:T(8,128)S(1)}, s32[12,3]{0,1:T(4,128)S(1)}, f32[12,1024]{1,0:T(8,128)S(1)}, s32[]{:T(128)}, /*index=5*/s32[]{:T(128)}) while((s32[]{:T(128)}, f32[1,12,1280]{2,1,0:T(8,128)S(1)}, s32[12,3]{0,1:T(4,128)S(1)}, f32[12,1024]{1,0:T(8,128)S(1)}, s32[]{:T(128)}, /*index=5*/s32[]{:T(128)}) %tuple.79), condition=%wide.while_cond, body=%wide.while_body.sunk | while | flops 2 | bytes 16509 | solution.py:77
  173.0 1.3 dynamic-slice_bitcast_fusion.10
  192.9 23.9 %while.17 = (s32[]{:T(128)}, f32[1,12,1216]{2,1,0:T(8,128)S(1)}, s32[12,3]{0,1:T(4,128)S(1)}, f32[12,1024]{1,0:T(8,128)S(1)}, s32[]{:T(128)}, /*index=5*/s32[]{:T(128)}) while((s32[]{:T(128)}, f32[1,12,1216]{2,1,0:T(8,128)S(1)}, s32[12,3]{0,1:T(4,128)S(1)}, f32[12,1024]{1,0:T(8,128)S(1)}, s32[]{:T(128)}, /*index=5*/s32[]{:T(128)}) %tuple.85), condition=%wide.while_cond.1, body=%wide.while_body.1.sunk | while | flops 2 | bytes 16509 | solution.py:77
  217.1 1.6 gather_fusion.1
  219.0 2.3 tile.14
  222.3 23.9 %while.18 = (s32[]{:T(128)}, f32[1,12,1280]{2,1,0:T(8,128)S(1)}, s32[12,3]{0,1:T(4,128)S(1)}, f32[12,1024]{1,0:T(8,128)S(1)}, s32[]{:T(128)}, /*index=5*/s32[]{:T(128)}) while((s32[]{:T(128)}, f32[1,12,1280]{2,1,0:T(8,128)S(1)}, s32[12,3]{0,1:T(4,128)S(1)}, f32[12,1024]{1,0:T(8,128)S(1)}, s32[]{:T(128)}, /*index=5*/s32[]{:T(128)}) %tuple.79), condition=%wide.while_cond, body=%wide.while_body.sunk | while | flops 2 | bytes 16509 | solution.py:77
  240.8 1.3 dynamic-slice_bitcast_fusion.10
  246.8 23.9 %while.17 = (s32[]{:T(128)}, f32[1,12,1216]{2,1,0:T(8,128)S(1)}, s32[12,3]{0,1:T(4,128)S(1)}, f32[12,1024]{1,0:T(8,128)S(1)}, s32[]{:T(128)}, /*index=5*/s32[]{:T(128)}) while((s32[]{:T(128)}, f32[1,12,1216]{2,1,0:T(8,128)S(1)}, s32[12,3]{0,1:T(4,128)S(1)}, f32[12,1024]{1,0:T(8,128)S(1)}, s32[]{:T(128)}, /*index=5*/s32[]{:T(128)}) %tuple.85), condition=%wide.while_cond.1, body=%wide.while_body.1.sunk | while | flops 2 | bytes 16509 | solution.py:77
  249.4 1.3 dynamic-slice_bitcast_fusion.9
  271.0 1.6 gather_fusion.1
  272.9 2.3 tile.14
  276.2 23.9 %while.18 = (s32[]{:T(128)}, f32[1,12,1280]{2,1,0:T(8,128)S(1)}, s32[12,3]{0,1:T(4,128)S(1)}, f32[12,1024]{1,0:T(8,128)S(1)}, s32[]{:T(128)}, /*index=5*/s32[]{:T(128)}) while((s32[]{:T(128)}, f32[1,12,1280]{2,1,0:T(8,128)S(1)}, s32[12,3]{0,1:T(4,128)S(1)}, f32[12,1024]{1,0:T(8,128)S(1)}, s32[]{:T(128)}, /*index=5*/s32[]{:T(128)}) %tuple.79), condition=%wide.while_cond, body=%wide.while_body.sunk | while | flops 2 | bytes 16509 | solution.py:77
  300.7 23.9 %while.17 = (s32[]{:T(128)}, f32[1,12,1216]{2,1,0:T(8,128)S(1)}, s32[12,3]{0,1:T(4,128)S(1)}, f32[12,1024]{1,0:T(8,128)S(1)}, s32[]{:T(128)}, /*index=5*/s32[]{:T(128)}) while((s32[]{:T(128)}, f32[1,12,1216]{2,1,0:T(8,128)S(1)}, s32[12,3]{0,1:T(4,128)S(1)}, f32[12,1024]{1,0:T(8,128)S(1)}, s32[]{:T(128)}, /*index=5*/s32[]{:T(128)}) %tuple.85), condition=%wide.while_cond.1, body=%wide.while_body.1.sunk | while | flops 2 | bytes 16509 | solution.py:77
  317.3 1.3 dynamic-slice_bitcast_fusion.9
  324.9 1.6 gather_fusion.1
  326.8 2.3 tile.14
  330.1 23.9 %while.18 = (s32[]{:T(128)}, f32[1,12,1280]{2,1,0:T(8,128)S(1)}, s32[12,3]{0,1:T(4,128)S(1)}, f32[12,1024]{1,0:T(8,128)S(1)}, s32[]{:T(128)}, /*index=5*/s32[]{:T(128)}) while((s32[]{:T(128)}, f32[1,12,1280]{2,1,0:T(8,128)S(1)}, s32[12,3]{0,1:T(4,128)S(1)}, f32[12,1024]{1,0:T(8,128)S(1)}, s32[]{:T(128)}, /*index=5*/s32[]{:T(128)}) %tuple.79), condition=%wide.while_cond, body=%wide.while_body.sunk | while | flops 2 | bytes 16509 | solution.py:77
  338.7 1.3 dynamic-slice_bitcast_fusion.10
  354.6 23.9 %while.17 = (s32[]{:T(128)}, f32[1,12,1216]{2,1,0:T(8,128)S(1)}, s32[12,3]{0,1:T(4,128)S(1)}, f32[12,1024]{1,0:T(8,128)S(1)}, s32[]{:T(128)}, /*index=5*/s32[]{:T(128)}) while((s32[]{:T(128)}, f32[1,12,1216]{2,1,0:T(8,128)S(1)}, s32[12,3]{0,1:T(4,128)S(1)}, f32[12,1024]{1,0:T(8,128)S(1)}, s32[]{:T(128)}, /*index=5*/s32[]{:T(128)}) %tuple.85), condition=%wide.while_cond.1, body=%wide.while_body.1.sunk | while | flops 2 | bytes 16509 | solution.py:77
  378.8 1.6 gather_fusion.1
  380.7 2.3 tile.14
  384.0 23.9 %while.18 = (s32[]{:T(128)}, f32[1,12,1280]{2,1,0:T(8,128)S(1)}, s32[12,3]{0,1:T(4,128)S(1)}, f32[12,1024]{1,0:T(8,128)S(1)}, s32[]{:T(128)}, /*index=5*/s32[]{:T(128)}) while((s32[]{:T(128)}, f32[1,12,1280]{2,1,0:T(8,128)S(1)}, s32[12,3]{0,1:T(4,128)S(1)}, f32[12,1024]{1,0:T(8,128)S(1)}, s32[]{:T(128)}, /*index=5*/s32[]{:T(128)}) %tuple.79), condition=%wide.while_cond, body=%wide.while_body.sunk | while | flops 2 | bytes 16509 | solution.py:77
  406.6 1.3 dynamic-slice_bitcast_fusion.10
  408.5 23.9 %while.17 = (s32[]{:T(128)}, f32[1,12,1216]{2,1,0:T(8,128)S(1)}, s32[12,3]{0,1:T(4,128)S(1)}, f32[12,1024]{1,0:T(8,128)S(1)}, s32[]{:T(128)}, /*index=5*/s32[]{:T(128)}) while((s32[]{:T(128)}, f32[1,12,1216]{2,1,0:T(8,128)S(1)}, s32[12,3]{0,1:T(4,128)S(1)}, f32[12,1024]{1,0:T(8,128)S(1)}, s32[]{:T(128)}, /*index=5*/s32[]{:T(128)}) %tuple.85), condition=%wide.while_cond.1, body=%wide.while_body.1.sunk | while | flops 2 | bytes 16509 | solution.py:77
  415.2 1.3 dynamic-slice_bitcast_fusion.9
  432.8 1.6 gather_fusion.1
  434.6 2.3 tile.14
  437.9 23.9 %while.18 = (s32[]{:T(128)}, f32[1,12,1280]{2,1,0:T(8,128)S(1)}, s32[12,3]{0,1:T(4,128)S(1)}, f32[12,1024]{1,0:T(8,128)S(1)}, s32[]{:T(128)}, /*index=5*/s32[]{:T(128)}) while((s32[]{:T(128)}, f32[1,12,1280]{2,1,0:T(8,128)S(1)}, s32[12,3]{0,1:T(4,128)S(1)}, f32[12,1024]{1,0:T(8,128)S(1)}, s32[]{:T(128)}, /*index=5*/s32[]{:T(128)}) %tuple.79), condition=%wide.while_cond, body=%wide.while_body.sunk | while | flops 2 | bytes 16509 | solution.py:77
  462.5 23.9 %while.17 = (s32[]{:T(128)}, f32[1,12,1216]{2,1,0:T(8,128)S(1)}, s32[12,3]{0,1:T(4,128)S(1)}, f32[12,1024]{1,0:T(8,128)S(1)}, s32[]{:T(128)}, /*index=5*/s32[]{:T(128)}) while((s32[]{:T(128)}, f32[1,12,1216]{2,1,0:T(8,128)S(1)}, s32[12,3]{0,1:T(4,128)S(1)}, f32[12,1024]{1,0:T(8,128)S(1)}, s32[]{:T(128)}, /*index=5*/s32[]{:T(128)}) %tuple.85), condition=%wide.while_cond.1, body=%wide.while_body.1.sunk | while | flops 2 | bytes 16509 | solution.py:77
  483.0 1.3 dynamic-slice_bitcast_fusion.9
  487.6 17.1 %all_to_all.5 = f32[32,2,1024]{2,1,0:T(2,128)S(1)} all-to-all(f32[32,2,1024]{2,1,0:T(2,128)S(1)} %reshape.276), channel_id=1, replica_groups=mesh['tm'=16,'chan'=32] {'chan'}, dimensions={0} | all-to-all | bytes 524288 | tf_op jit(solution)/shard_map/all_to_all | solution.py:119
  (960 shorter events, 373.2 us)
Async XLA Ops:
  0.8 16.3 %collective-permute-start = (bf16[16,1024]{1,0:T(8,128)(2,1)S(1)}, bf16[16,1024]{1,0:T(8,128)(2,1)S(1)}, u32[]{:S(2)}, u32[]{:S(2)}) collective-permute-start(bf16[16,1024]{1,0:T(8,128)(2,1)S(1)} %slice.59), channel_id=1, source_target_pairs={{0,31},{1,0},{2,1},{3,2},{4,3},{5,4},{6,5},{7,6},{8,7},{9,8},{10,9... | collective-permute-start | bytes 98312 | tf_op jit(solution)/shard_map/ppermute | solution.py:16
  17.1 22.9 %collective-permute-start.1 = (bf16[40,448]{1,0:T(8,128)(2,1)S(1)}, bf16[40,448]{1,0:T(8,128)(2,1)S(1)}, u32[]{:S(2)}, u32[]{:S(2)}) collective-permute-start(bf16[40,448]{1,0:T(8,128)(2,1)S(1)} %slice.105), channel_id=1, source_target_pairs={{0,480},{32,0},{64,32},{96,64},{128,96},{160,128},{192,160},{224,1... | collective-permute-start | bytes 107528 | tf_op jit(solution)/shard_map/ppermute | solution.py:16
  55.3 1.8 copy-start
  59.9 49.3 %copy-start.1 = (bf16[8,1,12,256]{3,2,1,0:T(8,128)(2,1)S(1)}, bf16[8,1,12,256]{3,2,1,0:T(8,128)(2,1)}, u32[]{:S(2)}) copy-start(bf16[8,1,12,256]{3,2,1,0:T(8,128)(2,1)} %copy-done) | copy-start | bytes 147460 | tf_op jit(solution)/shard_map/while
  109.2 1.8 copy-start
  113.8 49.3 %copy-start.1 = (bf16[8,1,12,256]{3,2,1,0:T(8,128)(2,1)S(1)}, bf16[8,1,12,256]{3,2,1,0:T(8,128)(2,1)}, u32[]{:S(2)}) copy-start(bf16[8,1,12,256]{3,2,1,0:T(8,128)(2,1)} %copy-done) | copy-start | bytes 147460 | tf_op jit(solution)/shard_map/while
  163.1 1.8 copy-start
  167.7 49.3 %copy-start.1 = (bf16[8,1,12,256]{3,2,1,0:T(8,128)(2,1)S(1)}, bf16[8,1,12,256]{3,2,1,0:T(8,128)(2,1)}, u32[]{:S(2)}) copy-start(bf16[8,1,12,256]{3,2,1,0:T(8,128)(2,1)} %copy-done) | copy-start | bytes 147460 | tf_op jit(solution)/shard_map/while
  217.0 1.8 copy-start
  221.6 49.3 %copy-start.1 = (bf16[8,1,12,256]{3,2,1,0:T(8,128)(2,1)S(1)}, bf16[8,1,12,256]{3,2,1,0:T(8,128)(2,1)}, u32[]{:S(2)}) copy-start(bf16[8,1,12,256]{3,2,1,0:T(8,128)(2,1)} %copy-done) | copy-start | bytes 147460 | tf_op jit(solution)/shard_map/while
  271.0 1.8 copy-start
  275.5 49.3 %copy-start.1 = (bf16[8,1,12,256]{3,2,1,0:T(8,128)(2,1)S(1)}, bf16[8,1,12,256]{3,2,1,0:T(8,128)(2,1)}, u32[]{:S(2)}) copy-start(bf16[8,1,12,256]{3,2,1,0:T(8,128)(2,1)} %copy-done) | copy-start | bytes 147460 | tf_op jit(solution)/shard_map/while
  324.9 1.8 copy-start
  329.5 49.3 %copy-start.1 = (bf16[8,1,12,256]{3,2,1,0:T(8,128)(2,1)S(1)}, bf16[8,1,12,256]{3,2,1,0:T(8,128)(2,1)}, u32[]{:S(2)}) copy-start(bf16[8,1,12,256]{3,2,1,0:T(8,128)(2,1)} %copy-done) | copy-start | bytes 147460 | tf_op jit(solution)/shard_map/while
  378.8 1.8 copy-start
  383.4 49.3 %copy-start.1 = (bf16[8,1,12,256]{3,2,1,0:T(8,128)(2,1)S(1)}, bf16[8,1,12,256]{3,2,1,0:T(8,128)(2,1)}, u32[]{:S(2)}) copy-start(bf16[8,1,12,256]{3,2,1,0:T(8,128)(2,1)} %copy-done) | copy-start | bytes 147460 | tf_op jit(solution)/shard_map/while
  432.7 1.8 copy-start
  437.3 49.3 %copy-start.1 = (bf16[8,1,12,256]{3,2,1,0:T(8,128)(2,1)S(1)}, bf16[8,1,12,256]{3,2,1,0:T(8,128)(2,1)}, u32[]{:S(2)}) copy-start(bf16[8,1,12,256]{3,2,1,0:T(8,128)(2,1)} %copy-done) | copy-start | bytes 147460 | tf_op jit(solution)/shard_map/while
where the time goes:
time: 509 us; the launch traced here: 506 us
  local copies, waits for them, and re-layouts  430 us (84%)
  blocking collectives  36.5 us (7%)
  starting transfers between devices  14.6 us (3%)
  other arithmetic  14.5 us (3%)
  loops' own time  6.1 us (1%)
    gather x768, local copies, waits for them, and re-layouts  378 us
    all_gather x1, blocking collectives, local(): full_waves = lax.all_gather(template_waves, 'tm', axis=2, tiled=True)  19.4 us
    another operation x24, local copies, waits for them, and re-layouts, one_template(): jnp.tile(padded_wave, (1, BLOCK))[:, :BLOCK * frame_width]  19.2 us
    all_to_all x1, blocking collectives, local(): lax.all_to_all(outgoing, 'chan', split_axis=0, concat_axis=0, tiled=True)  17.1 us
    ppermute x2, starting transfers between devices, passed_along(): return lax.ppermute(value, axis, pairs)  14.6 us
    gather x8, local copies, waits for them, and re-layouts, one_template(): framed = frames[rows_t]  12.9 us
  transfers between devices with their start and end apart: 2, of which 0 were waited for; matrix products, arithmetic and copies ran while one was open for 1% of the time, Pallas kernels for 0%

commit v1 on v0

v1 whole, which is shorter than its diff:
```python
import jax
import jax.numpy as jnp
from jax import lax
from jax.experimental import pallas as pl
from jax.experimental.pallas import tpu as pltpu
from jax.sharding import PartitionSpec as P

L = 256
SLOTS = 12
SPILL = 16
LANES = 128
ROWS = 16
HALO = 512
TPL = 8
CH = 24
SCAP = 2
F32 = jnp.float32
BF16 = jnp.bfloat16


def shift_pairs(count, steps):
    return [(source, (source + steps) % count) for source in range(count)]


def stack_kernel(total_chan, tab, rec, right, down, diag, waves, out, xs, xx, ee, pr, wr, we, sh):
    group = lax.axis_index("chan")
    rows_all = (CH + SPILL) * ROWS

    xs[...] = jnp.zeros_like(xs)
    for b in range(8):
        cut = slice(LANES * b, LANES * (b + 1))
        xs[pl.ds(b, CH, stride=ROWS), :] = rec[:, cut].astype(F32)
        xs[pl.ds(CH * ROWS + b, SPILL, stride=ROWS), :] = down[:, cut].astype(F32)
    for b in range(4):
        cut = slice(LANES * b, LANES * (b + 1))
        xs[pl.ds(8 + b, CH, stride=ROWS), :] = right[:, cut].astype(F32)
        xs[pl.ds(CH * ROWS + 8 + b, SPILL, stride=ROWS), :] = diag[:, cut].astype(F32)

    row_id = lax.broadcasted_iota(jnp.int32, (LANES, LANES), 0)
    lane_id = lax.broadcasted_iota(jnp.int32, (LANES, LANES), 1)
    lower = jnp.where(row_id >= lane_id, 1.0, 0.0).astype(BF16)
    upper = jnp.where(row_id < lane_id, 1.0, 0.0).astype(BF16)
    tri = jnp.concatenate([lower, upper], axis=1)
    ones_band = jnp.concatenate([tri, tri], axis=0)

    now = xs[pl.ds(0, rows_all), :]
    nxt = xs[pl.ds(1, rows_all), :]
    pair = jnp.concatenate([now, nxt], axis=1)
    xx[...] = pair.astype(BF16)
    square = pair * pair
    high = square.astype(BF16)
    low = (square - high.astype(F32)).astype(BF16)
    both = jnp.dot(high, ones_band, preferred_element_type=F32) + jnp.dot(
        low, ones_band, preferred_element_type=F32
    )
    pr[pl.ds(0, rows_all), :] = both[:, LANES:]
    ee[...] = both[:, :LANES] + pr[pl.ds(1, rows_all), :]

    wave_t = waves[...].astype(F32).T
    sample_id = lax.broadcasted_iota(jnp.int32, (L, L), 0)
    place_id = lax.broadcasted_iota(jnp.int32, (L, L), 1)
    same_half = (sample_id >= LANES) == (place_id >= LANES)
    mirrored = ((sample_id + place_id) & (LANES - 1)) == 0
    turn = jnp.where(same_half & mirrored, 1.0, 0.0).astype(BF16)
    turned = jnp.dot(wave_t.astype(BF16), turn, preferred_element_type=F32)
    wr[0] = turned[:, :LANES]
    wr[1] = turned[:, LANES:]
    we[...] = jnp.broadcast_to(jnp.sum(wave_t * wave_t, axis=1, keepdims=True), we.shape)

    out[...] = jnp.zeros_like(out)
    lane_row = lax.broadcasted_iota(jnp.int32, (TPL, LANES), 1)

    def circulant(p, half):
        row = wr[half, pl.ds(p, 1), :]
        full = jnp.broadcast_to(row, (LANES, LANES))
        return pltpu.roll(full, 0, 1, stride=1, stride_axis=0).astype(BF16)

    def one_template(k, carry):
        total = jnp.zeros((TPL, LANES), F32)
        for j in range(SLOTS):
            p = k * SLOTS + j
            listed = tab[k, j]
            valid = listed >= 0
            place = listed - group * CH
            place = jnp.where(place < 0, place + total_chan, place)
            place = jnp.where(valid, place, 0)
            start = pl.multiple_of(place * ROWS, ROWS)
            shift = tab[k, SLOTS + j]
            lanes, rows = shift & (LANES - 1), shift >> 7
            first, second = circulant(p, 0), circulant(p, 1)
            band = jnp.concatenate(
                [
                    jnp.concatenate([first * lower, first * upper], axis=1),
                    jnp.concatenate([second * lower, second * upper], axis=1),
                ],
                axis=0,
            )
            prod = jnp.dot(xx[pl.ds(start, ROWS), :], band, preferred_element_type=F32)
            corr = prod[:, :LANES] + pltpu.roll(prod[:, LANES:], ROWS - 1, 0)
            scale = we[pl.ds(p, 1), :] * ee[pl.ds(start, ROWS), :] + 1e-06
            normed = corr * lax.rsqrt(scale)
            sh[j] = pltpu.roll(normed, (LANES - lanes) & (LANES - 1), 1)
            here = sh[j, pl.ds(rows, TPL), :]
            after = sh[j, pl.ds(rows + 1, TPL), :]
            moved = jnp.where(lane_row < LANES - lanes, here, after)
            total = total + jnp.where(valid, moved, 0.0)
        owner = tab[k, 2 * SLOTS]
        rank = jnp.int32(0)
        for q in range(TPL):
            same = (tab[q, 2 * SLOTS] == owner) & (q < k)
            rank = rank + jnp.where(same, 1, 0)
        out[owner * SCAP + rank] = total
        return carry

    lax.fori_loop(0, TPL, one_template, 0)


def local(records, template_waves, channel_lists, moveouts, owner_map):
    ch_dev, t_dev = records.shape
    n_chan = lax.axis_size("chan")
    n_tm = lax.axis_size("tm")
    total_chan = ch_dev * n_chan
    group = lax.axis_index("chan")

    pairs_n = TPL * SLOTS
    own = template_waves.reshape(pairs_n, L // n_tm).T
    own = jnp.pad(own, ((0, 0), (0, LANES - pairs_n)))
    waves = lax.all_to_all(
        jnp.broadcast_to(own[None], (n_tm, L // n_tm, LANES)), "tm", 0, 0
    ).reshape(L, LANES)
    right = lax.ppermute(records[:, :HALO], "tm", shift_pairs(n_tm, -1))
    down = lax.ppermute(records[:SPILL], "chan", shift_pairs(n_chan, -1))
    across = [
        (t * n_chan + g, (t - 1) % n_tm * n_chan + (g - 1) % n_chan)
        for t in range(n_tm)
        for g in range(n_chan)
    ]
    diag = lax.ppermute(records[:SPILL, :HALO], ("tm", "chan"), across)
    table = jnp.concatenate([channel_lists, moveouts, owner_map], axis=1)
    table = lax.dynamic_slice_in_dim(table, group * TPL, TPL, 0)

    rows_all = (CH + SPILL) * ROWS
    vmem = pl.BlockSpec(memory_space=pltpu.VMEM)
    outgoing = pl.pallas_call(
        lambda *refs: stack_kernel(total_chan, *refs),
        out_shape=jax.ShapeDtypeStruct((n_chan * SCAP, TPL, LANES), F32),
        in_specs=[pl.BlockSpec(memory_space=pltpu.SMEM)] + [vmem] * 5,
        out_specs=vmem,
        scratch_shapes=[
            pltpu.VMEM((rows_all + 8, LANES), F32),
            pltpu.VMEM((rows_all, 2 * LANES), BF16),
            pltpu.VMEM((rows_all, LANES), F32),
            pltpu.VMEM((rows_all + 8, LANES), F32),
            pltpu.VMEM((2, LANES, LANES), F32),
            pltpu.VMEM((LANES, LANES), F32),
            pltpu.VMEM((SLOTS, ROWS, LANES), F32),
        ],
        compiler_params=pltpu.CompilerParams(vmem_limit_bytes=32 * 1024 * 1024),
    )(table, records, right, down, diag, waves)
    incoming = lax.all_to_all(
        outgoing.reshape(n_chan, SCAP, TPL, LANES), "chan", 0, 0
    )
    return incoming.reshape(n_chan * SCAP, t_dev)


def solution(mesh):
    in_specs = (P("chan", "tm"), P("chan", None, "tm"), P(), P(), P())
    out_specs = P("chan", "tm")
    return jax.shard_map(local, mesh=mesh, in_specs=in_specs, out_specs=out_specs, check_vma=False)
```

time: 509 us -> 53.4 us (0.10)
  the two profiles are of different devices: /device:TPU:1 before, /device:TPU:6 now
where the time goes in v1:
time: 53.4 us; the launch traced here: 53 us
  blocking collectives  24.5 us (46%)
  starting transfers between devices  15.5 us (29%)
  Pallas kernels  5.1 us (10%)
  waiting for transfers between devices  4.63 us (9%)
  local copies, waits for them, and re-layouts  3.13 us (6%)
    all_to_all x1, blocking collectives, local(): lax.all_to_all(outgoing.reshape(n_chan, SCAP, TPL, LANES), 'chan', 0, 0)  24.5 us
    all_to_all x1, starting transfers between devices, local(): lax.all_to_all(jnp.broadcast_to(own[None], (n_tm, L // n_tm, LANES)), 'tm...  7.34 us
    pallas_call x1, Pallas kernels, local(): pl.pallas_call(lambda *refs: stack_kernel(total_chan, *refs), out_shape=j...  5.1 us
    ppermute x1, starting transfers between devices, local(): diag = lax.ppermute(records[:SPILL, :HALO], ('tm', 'chan'), across)  5.07 us
    ppermute x1, waiting for transfers between devices, local(): down = lax.ppermute(records[:SPILL], 'chan', shift_pairs(n_chan, -1))  4.62 us
    ppermute x1, starting transfers between devices, local(): down = lax.ppermute(records[:SPILL], 'chan', shift_pairs(n_chan, -1))  2.57 us
    unnamed x11, local copies, waits for them, and re-layouts  2.37 us
  transfers between devices with their start and end apart: 4, of which 1 were waited for; matrix products, arithmetic and copies ran while one was open for 0% of the time, Pallas kernels for 0%

profile of v1, /device:TPU:6, one launch (start us, length us, event | category | flops | bytes accessed | tf_op | source)
XLA Modules:
  0.0 53.0 jit_solution(18108435604734279318)
XLA Ops:
  0.0 0.9 %copy.14 = bf16[8,12,16]{1,0,2:T(8,128)(2,1)S(1)} copy(bf16[8,12,16]{2,0,1:T(8,128)(2,1)} %param.6) | data formatting | bytes 6144 | tf_op args[1]
  0.9 0.1 reshape.13
  1.0 0.6 %broadcast_in_dim.2 = bf16[16,16,128]{2,1,0:T(8,128)(2,1)} broadcast(bf16[16,128]{1,0:T(8,128)(2,1)S(1)} %pad.4), dimensions={1,2} | broadcast | bytes 69632 | tf_op jit(solution)/shard_map/broadcast_in_dim | solution.py:129
  1.6 0.0 copy-start
  1.6 7.3 %all-to-all-start = ((bf16[16,16,128]{2,1,0:T(8,128)(2,1)}), bf16[16,16,128]{2,1,0:T(8,128)(2,1)S(1)}, u32[]{:S(2)}, u32[]{:S(2)}) async-start(bf16[16,16,128]{2,1,0:T(8,128)(2,1)} %broadcast_in_dim.2), calls=%async_computation | async-start | bytes 131072 | tf_op jit(solution)/shard_map/all_to_all | solution.py:128
  9.0 0.0 copy-done
  9.0 5.1 %collective-permute-start.2 = (bf16[16,512]{1,0:T(8,128)(2,1)S(1)}, bf16[16,512]{1,0:T(8,128)(2,1)S(1)}, u32[]{:S(2)}, u32[]{:S(2)}) collective-permute-start(bf16[16,512]{1,0:T(8,128)(2,1)S(1)} %slice.11), channel_id=1, source_target_pairs={{0,511},{1,480},{2,481},{3,482},{4,483},{5,484},{6,485},{7,486},{8... | collective-permute-start | bytes 49160 | tf_op jit(solution)/shard_map/ppermute | solution.py:138
  14.1 0.5 %collective-permute-start = (bf16[24,512]{1,0:T(8,128)(2,1)S(1)}, bf16[24,512]{1,0:T(8,128)(2,1)S(1)}, u32[]{:S(2)}, u32[]{:S(2)}) collective-permute-start(bf16[24,512]{1,0:T(8,128)(2,1)S(1)} %slice.9), channel_id=1, source_target_pairs={{0,480},{32,0},{64,32},{96,64},{128,96},{160,128},{192,160},{224,1... | collective-permute-start | bytes 73736 | tf_op jit(solution)/shard_map/ppermute | solution.py:131
  14.6 0.0 copy-start.1
  14.6 0.0 copy-start.2
  14.6 2.6 %collective-permute-start.1 = (bf16[16,1024]{1,0:T(8,128)(2,1)S(1)}, bf16[16,1024]{1,0:T(8,128)(2,1)S(1)}, u32[]{:S(2)}, u32[]{:S(2)}) collective-permute-start(bf16[16,1024]{1,0:T(8,128)(2,1)S(1)} %slice.10), channel_id=1, source_target_pairs={{0,31},{1,0},{2,1},{3,2},{4,3},{5,4},{6,5},{7,6},{8,7},{9,8},{10,9... | collective-permute-start | bytes 98312 | tf_op jit(solution)/shard_map/ppermute | solution.py:132
  17.2 0.0 copy-start.3
  17.2 0.0 copy-done.1
  17.2 0.0 copy-done.2
  17.2 0.7 %copy-done.3 = s32[256,1]{0,1:T(1,128)S(1)} copy-done((s32[256,1]{0,1:T(1,128)S(1)}, s32[256,1]{0,1:T(1,128)}, u32[]{:S(2)}) %copy-start.3) | copy-done | bytes 1048
  17.9 0.1 fusion.1
  18.0 0.1 copy.15.refs_0_
  18.1 0.0 collective-permute-done.2.refs_4_
  18.1 0.0 collective-permute-done.refs_2_
  18.1 4.6 %collective-permute-done.1.refs_3_ = bf16[16,1024]{1,0:T(8,128)(2,1)S(1)} collective-permute-done((bf16[16,1024]{1,0:T(8,128)(2,1)S(1)}, bf16[16,1024]{1,0:T(8,128)(2,1)S(1)}, u32[]{:S(2)}, u32[]{:S(2)}) %collective-permute-start.1) | collective-permute-done | bytes 32800 | tf_op jit(solution)/shard_map/ppermute | solution.py:132
  22.7 0.0 all-to-all-done
  22.7 5.1 %shard_map.55 = f32[64,8,128]{2,1,0:T(8,128)S(1)} custom-call(s32[8,25]{1,0:T(8,128)S(1)} %copy.15.refs_0_, bf16[24,1024]{1,0:T(8,128)(2,1)S(1)} %copy-done, bf16[24,512]{1,0:T(8,128)(2,1)S(1)} %collective-permute-done.refs_2_, bf16[16,1024]{1,0:T(8,128)(2,1)S(1)} %collective-permute-done.1.refs_3_, bf16[16,512]{1,0:T(8,128)(2,1)S(1)} %collective-permute-done.2.refs_4_, ...), custom_call_target="tpu_custom_call" | custom-call | tf_op jit(solution)/shard_map/pallas_call | solution.py:144
  27.8 24.5 %all_to_all.10 = f32[32,2,8,128]{3,2,1,0:T(8,128)S(1)} all-to-all(f32[32,2,8,128]{3,2,1,0:T(8,128)S(1)} %bitcast.10), channel_id=1, replica_groups=mesh['tm'=16,'chan'=32] {'chan'}, dimensions={0} | all-to-all | bytes 524288 | tf_op jit(solution)/shard_map/all_to_all | solution.py:160
  52.2 0.8 %copy.18 = f32[8,8,8,128]{3,1,2,0:T(8,128)} copy(f32[8,8,8,128]{3,2,1,0:T(8,128)S(1)} %bitcast.12) | data formatting | bytes 524288
  (4 shorter events, 0.0 us)
Async XLA Ops:
  1.6 7.3 %copy-start = (bf16[24,1024]{1,0:T(8,128)(2,1)S(1)}, bf16[24,1024]{1,0:T(8,128)(2,1)}, u32[]{:S(2)}) copy-start(bf16[24,1024]{1,0:T(8,128)(2,1)} %refs_1_.1) | copy-start | bytes 147460
  1.6 21.0 %all-to-all-start = ((bf16[16,16,128]{2,1,0:T(8,128)(2,1)}), bf16[16,16,128]{2,1,0:T(8,128)(2,1)S(1)}, u32[]{:S(2)}, u32[]{:S(2)}) async-start(bf16[16,16,128]{2,1,0:T(8,128)(2,1)} %broadcast_in_dim.2), calls=%async_computation | async-start | bytes 131072 | tf_op jit(solution)/shard_map/all_to_all | solution.py:128
  9.0 9.1 %collective-permute-start.2 = (bf16[16,512]{1,0:T(8,128)(2,1)S(1)}, bf16[16,512]{1,0:T(8,128)(2,1)S(1)}, u32[]{:S(2)}, u32[]{:S(2)}) collective-permute-start(bf16[16,512]{1,0:T(8,128)(2,1)S(1)} %slice.11), channel_id=1, source_target_pairs={{0,511},{1,480},{2,481},{3,482},{4,483},{5,484},{6,485},{7,486},{8... | collective-permute-start | bytes 49160 | tf_op jit(solution)/shard_map/ppermute | solution.py:138
  14.1 4.0 %collective-permute-start = (bf16[24,512]{1,0:T(8,128)(2,1)S(1)}, bf16[24,512]{1,0:T(8,128)(2,1)S(1)}, u32[]{:S(2)}, u32[]{:S(2)}) collective-permute-start(bf16[24,512]{1,0:T(8,128)(2,1)S(1)} %slice.9), channel_id=1, source_target_pairs={{0,480},{32,0},{64,32},{96,64},{128,96},{160,128},{192,160},{224,1... | collective-permute-start | bytes 73736 | tf_op jit(solution)/shard_map/ppermute | solution.py:131
  14.6 2.6 %copy-start.1 = (s32[256,12]{0,1:T(8,128)S(1)}, s32[256,12]{0,1:T(8,128)}, u32[]{:S(2)}) copy-start(s32[256,12]{0,1:T(8,128)} %param.7) | copy-start | bytes 36868
  14.6 2.6 %copy-start.2 = (s32[256,12]{0,1:T(8,128)S(1)}, s32[256,12]{0,1:T(8,128)}, u32[]{:S(2)}) copy-start(s32[256,12]{0,1:T(8,128)} %param.8) | copy-start | bytes 36868
  14.6 8.0 %collective-permute-start.1 = (bf16[16,1024]{1,0:T(8,128)(2,1)S(1)}, bf16[16,1024]{1,0:T(8,128)(2,1)S(1)}, u32[]{:S(2)}, u32[]{:S(2)}) collective-permute-start(bf16[16,1024]{1,0:T(8,128)(2,1)S(1)} %slice.10), channel_id=1, source_target_pairs={{0,31},{1,0},{2,1},{3,2},{4,3},{5,4},{6,5},{7,6},{8,7},{9,8},{10,9... | collective-permute-start | bytes 98312 | tf_op jit(solution)/shard_map/ppermute | solution.py:132
  17.2 0.7 %copy-start.3 = (s32[256,1]{0,1:T(1,128)S(1)}, s32[256,1]{0,1:T(1,128)}, u32[]{:S(2)}) copy-start(s32[256,1]{0,1:T(1,128)} %param.9) | copy-start | bytes 3076

commit v2 on v1

v2 whole, which is shorter than its diff:
```python
import jax
import jax.numpy as jnp
from jax import lax
from jax.experimental import pallas as pl
from jax.experimental.pallas import tpu as pltpu
from jax.sharding import PartitionSpec as P

L = 256
SLOTS = 12
SPILL = 16
LANES = 128
ROWS = 16
HALO = 512
TPL = 8
CH = 24
SCAP = 2
PAIRS = TPL * SLOTS
ALL_ROWS = (CH + SPILL) * ROWS
F32 = jnp.float32
BF16 = jnp.bfloat16


def chunk_kernel(waves, out):
    rows = [waves[j].astype(F32) for j in range(SLOTS)]
    flat = jnp.concatenate(rows + [jnp.zeros((LANES - PAIRS, rows[0].shape[1]), F32)], axis=0)
    wide = jnp.concatenate([flat, jnp.zeros((LANES, LANES - flat.shape[1]), F32)], axis=1)
    turned = wide.T[: out.shape[1]].astype(BF16)
    for i in range(out.shape[0]):
        out[i] = turned


def frame_kernel(rec, right, below, xx, ee, xs, pr):
    for b in range(8):
        cut = slice(LANES * b, LANES * (b + 1))
        xs[pl.ds(b, CH, stride=ROWS), :] = rec[:, cut].astype(F32)
    for b in range(4):
        cut = slice(LANES * b, LANES * (b + 1))
        xs[pl.ds(8 + b, CH, stride=ROWS), :] = right[:, cut].astype(F32)
        xs[pl.ds(12 + b, CH + SPILL, stride=ROWS), :] = jnp.zeros((CH + SPILL, LANES), F32)
    for b in range(12):
        cut = slice(LANES * b, LANES * (b + 1))
        xs[pl.ds(CH * ROWS + b, SPILL, stride=ROWS), :] = below[:, cut].astype(F32)
    xs[pl.ds(ALL_ROWS, 8), :] = jnp.zeros((8, LANES), F32)

    row_id = lax.broadcasted_iota(jnp.int32, (LANES, LANES), 0)
    lane_id = lax.broadcasted_iota(jnp.int32, (LANES, LANES), 1)
    lower = jnp.where(row_id >= lane_id, 1.0, 0.0).astype(BF16)
    upper = jnp.where(row_id < lane_id, 1.0, 0.0).astype(BF16)
    tri = jnp.concatenate([lower, upper], axis=1)
    ones_band = jnp.concatenate([tri, tri], axis=0)

    now = xs[pl.ds(0, ALL_ROWS), :]
    nxt = xs[pl.ds(1, ALL_ROWS), :]
    pair = jnp.concatenate([now, nxt], axis=1)
    xx[...] = pair.astype(BF16)
    square = pair * pair
    high = square.astype(BF16)
    low = (square - high.astype(F32)).astype(BF16)
    both = jnp.dot(high, ones_band, preferred_element_type=F32) + jnp.dot(
        low, ones_band, preferred_element_type=F32
    )
    pr[pl.ds(0, ALL_ROWS), :] = both[:, LANES:]
    pr[pl.ds(ALL_ROWS, 8), :] = jnp.zeros((8, LANES), F32)
    ee[...] = both[:, :LANES] + pr[pl.ds(1, ALL_ROWS), :]


def stack_kernel(total_chan, lists, moves, owners, xx, ee, waves, out, wr, we, sh):
    group = lax.axis_index("chan")
    wave_t = waves[...].astype(F32).T
    sample_id = lax.broadcasted_iota(jnp.int32, (L, L), 0)
    place_id = lax.broadcasted_iota(jnp.int32, (L, L), 1)
    same_half = (sample_id >= LANES) == (place_id >= LANES)
    mirrored = ((sample_id + place_id) & (LANES - 1)) == 0
    turn = jnp.where(same_half & mirrored, 1.0, 0.0).astype(BF16)
    turned = jnp.dot(wave_t.astype(BF16), turn, preferred_element_type=F32)
    wr[0] = turned[:, :LANES]
    wr[1] = turned[:, LANES:]
    we[...] = jnp.broadcast_to(jnp.sum(wave_t * wave_t, axis=1, keepdims=True), we.shape)

    out[...] = jnp.zeros_like(out)
    lane_row = lax.broadcasted_iota(jnp.int32, (TPL, LANES), 1)
    row_id = lax.broadcasted_iota(jnp.int32, (LANES, LANES), 0)
    lane_id = lax.broadcasted_iota(jnp.int32, (LANES, LANES), 1)
    lower = jnp.where(row_id >= lane_id, 1.0, 0.0).astype(BF16)
    upper = jnp.where(row_id < lane_id, 1.0, 0.0).astype(BF16)

    def circulant(p, half):
        row = wr[half, pl.ds(p, 1), :]
        full = jnp.broadcast_to(row, (LANES, LANES)).astype(BF16)
        return pltpu.roll(full, 0, 1, stride=1, stride_axis=0)

    def one_template(k, carry):
        total = jnp.zeros((TPL, LANES), F32)
        tpl = group * TPL + k
        for j in range(SLOTS):
            p = j * TPL + k
            listed = lists[j, tpl]
            valid = listed >= 0
            place = listed - group * CH
            place = jnp.where(place < 0, place + total_chan, place)
            place = jnp.where(valid, place, 0)
            start = pl.multiple_of(place * ROWS, ROWS)
            shift = moves[j, tpl]
            lanes, rows = shift & (LANES - 1), shift >> 7
            first, second = circulant(p, 0), circulant(p, 1)
            band = jnp.concatenate(
                [
                    jnp.concatenate([first * lower, first * upper], axis=1),
                    jnp.concatenate([second * lower, second * upper], axis=1),
                ],
                axis=0,
            )
            prod = jnp.dot(xx[pl.ds(start, ROWS), :], band, preferred_element_type=F32)
            corr = prod[:, :LANES] + pltpu.roll(prod[:, LANES:], ROWS - 1, 0)
            scale = we[pl.ds(p, 1), :] * ee[pl.ds(start, ROWS), :] + 1e-06
            normed = corr * lax.rsqrt(scale)
            sh[j] = pltpu.roll(normed, (LANES - lanes) & (LANES - 1), 1)
            here = sh[j, pl.ds(rows, TPL), :]
            after = sh[j, pl.ds(rows + 1, TPL), :]
            moved = jnp.where(lane_row < LANES - lanes, here, after)
            total = total + jnp.where(valid, moved, 0.0)
        owner = owners[0, tpl]
        rank = jnp.int32(0)
        for q in range(TPL):
            same = (owners[0, group * TPL + q] == owner) & (q < k)
            rank = rank + jnp.where(same, 1, 0)
        out[owner * SCAP + rank] = total
        return carry

    lax.fori_loop(0, TPL, one_template, 0, unroll=True)


def shifted(value, axis, count):
    return lax.ppermute(value, axis, [(s, (s - 1) % count) for s in range(count)])


def gathered(chunks):
    return lax.all_to_all(chunks, "tm", 0, 0).reshape(L, LANES)


def local(records, template_waves, channel_lists, moveouts, owner_map):
    ch_dev, t_dev = records.shape
    n_chan = lax.axis_size("chan")
    n_tm = lax.axis_size("tm")
    vmem = pl.BlockSpec(memory_space=pltpu.VMEM)
    smem = pl.BlockSpec(memory_space=pltpu.SMEM)
    params = pltpu.CompilerParams(vmem_limit_bytes=24 * 1024 * 1024)

    chunks = pl.pallas_call(
        chunk_kernel,
        out_shape=jax.ShapeDtypeStruct((n_tm, L // n_tm, LANES), BF16),
        in_specs=[vmem],
        out_specs=vmem,
        compiler_params=params,
    )(jnp.transpose(template_waves, (1, 0, 2)))
    right = shifted(records[:, :HALO], "tm", n_tm)
    edge = jnp.concatenate([records[:SPILL], right[:SPILL]], axis=1)
    below = shifted(edge, "chan", n_chan)
    waves = gathered(chunks)
    frames, energy = pl.pallas_call(
        frame_kernel,
        out_shape=(
            jax.ShapeDtypeStruct((ALL_ROWS, 2 * LANES), BF16),
            jax.ShapeDtypeStruct((ALL_ROWS, LANES), F32),
        ),
        in_specs=[vmem] * 3,
        out_specs=(vmem, vmem),
        scratch_shapes=[
            pltpu.VMEM((ALL_ROWS + 8, LANES), F32),
            pltpu.VMEM((ALL_ROWS + 8, LANES), F32),
        ],
        compiler_params=params,
        cost_estimate=pl.CostEstimate(flops=200_000_000, bytes_accessed=1_000_000, transcendentals=0),
    )(records, right, below)
    outgoing = pl.pallas_call(
        lambda *refs: stack_kernel(ch_dev * n_chan, *refs),
        out_shape=jax.ShapeDtypeStruct((n_chan * SCAP, TPL, LANES), F32),
        in_specs=[smem] * 3 + [vmem] * 3,
        out_specs=vmem,
        scratch_shapes=[
            pltpu.VMEM((2, LANES, LANES), F32),
            pltpu.VMEM((LANES, LANES), F32),
            pltpu.VMEM((SLOTS, ROWS, LANES), F32),
        ],
        compiler_params=params,
    )(channel_lists.T, moveouts.T, owner_map.T, frames, energy, waves)
    incoming = lax.all_to_all(outgoing.reshape(n_chan, SCAP, TPL, LANES), "chan", 0, 0)
    return incoming.reshape(n_chan * SCAP, t_dev)


def solution(mesh):
    in_specs = (P("chan", "tm"), P("chan", None, "tm"), P(), P(), P())
    out_specs = P("chan", "tm")
    return jax.shard_map(local, mesh=mesh, in_specs=in_specs, out_specs=out_specs, check_vma=False)
```

time: 53.4 us -> 50.2 us (0.940)
  the two profiles are of different devices: /device:TPU:6 before, /device:TPU:8 now
where the time goes in v2:
time: 50.2 us; the launch traced here: 49.8 us
  starting transfers between devices  20.9 us (42%)
  blocking collectives  19.5 us (39%)
  Pallas kernels  4.65 us (9%)
  local copies, waits for them, and re-layouts  2.92 us (6%)
  waiting for transfers between devices  1.73 us (3%)
    all_to_all x1, blocking collectives, local(): lax.all_to_all(outgoing.reshape(n_chan, SCAP, TPL, LANES), 'chan', 0, 0)  19.5 us
    ppermute x2, starting transfers between devices, shifted(): lax.ppermute(value, axis, [(s, (s - 1) % count) for s in range(count)])  11.8 us
    all_to_all x1, starting transfers between devices, gathered(): return lax.all_to_all(chunks, 'tm', 0, 0).reshape(L, LANES)  9.12 us
    pallas_call x1, Pallas kernels, local(): pl.pallas_call(lambda *refs: stack_kernel(ch_dev * n_chan, *refs), out_sh...  3.46 us
    ppermute x2, waiting for transfers between devices, shifted(): lax.ppermute(value, axis, [(s, (s - 1) % count) for s in range(count)])  1.73 us
    unnamed x11, local copies, waits for them, and re-layouts  1.44 us
  transfers between devices with their start and end apart: 3, of which 1 were waited for; matrix products, arithmetic and copies ran while one was open for 0% of the time, Pallas kernels for 2%

profile of v2, /device:TPU:8, one launch (start us, length us, event | category | flops | bytes accessed | tf_op | source)
XLA Modules:
  0.0 49.8 jit_solution(14879988335280489573)
XLA Ops:
  0.0 0.0 copy-start.1
  0.0 0.7 %slice.9 = bf16[24,512]{1,0:T(8,128)(2,1)S(1)} slice(bf16[24,1024]{1,0:T(8,128)(2,1)} %rec.1), slice={[0:24], [0:512]} | slice | bytes 49152 | tf_op jit(solution)/shard_map/slice | solution.py:156
  0.7 0.0 collective-permute-start
  0.8 0.0 copy-done.1
  0.8 0.7 %shard_map.56 = bf16[16,16,128]{2,1,0:T(8,128)(2,1)} custom-call(bf16[12,8,16]{2,1,0:T(8,128)(2,1)S(1)} %bitcast.13), custom_call_target="tpu_custom_call" | custom-call | tf_op jit(solution)/shard_map/pallas_call | solution.py:149
  1.5 9.1 %all-to-all-start = ((bf16[16,16,128]{2,1,0:T(8,128)(2,1)}), bf16[16,16,128]{2,1,0:T(8,128)(2,1)S(1)}, u32[]{:S(2)}, u32[]{:S(2)}) async-start(bf16[16,16,128]{2,1,0:T(8,128)(2,1)} %shard_map.56), calls=%async_computation | async-start | bytes 131072 | tf_op jit(solution)/shard_map/all_to_all | solution.py:138
  10.6 0.0 slice-start
  10.6 0.0 collective-permute-done.right
  10.6 0.7 %slice-done = bf16[16,1024]{1,0:T(8,128)(2,1)S(1)} async-done(((bf16[24,1024]{1,0:T(8,128)(2,1)}), bf16[16,1024]{1,0:T(8,128)(2,1)S(1)}, s32[]{:S(2)}) %slice-start) | async-done | bytes 32792 | tf_op jit(solution)/shard_map/slice | solution.py:157
  11.3 0.0 copy-start
  11.3 11.8 %collective-permute-start.1 = (bf16[16,1536]{1,0:T(8,128)(2,1)S(1)}, bf16[16,1536]{1,0:T(8,128)(2,1)S(1)}, u32[]{:S(2)}, u32[]{:S(2)}) collective-permute-start(bf16[16,1536]{1,0:T(8,128)(2,1)S(1)} %pad_maximum_fusion), channel_id=1, source_target_pairs={{0,31},{1,0},{2,1},{3,2},{4,3},{5,4},{6,5},{7,6},{8,7},{9,8},{10,9... | collective-permute-start | bytes 147464 | tf_op jit(solution)/shard_map/ppermute | solution.py:134
  23.2 1.7 %collective-permute-done.1.below = bf16[16,1536]{1,0:T(8,128)(2,1)S(1)} collective-permute-done((bf16[16,1536]{1,0:T(8,128)(2,1)S(1)}, bf16[16,1536]{1,0:T(8,128)(2,1)S(1)}, u32[]{:S(2)}, u32[]{:S(2)}) %collective-permute-start.1) | collective-permute-done | bytes 49184 | tf_op jit(solution)/shard_map/ppermute | solution.py:134
  24.9 0.0 copy-done
  24.9 0.0 copy-start.2
  24.9 0.0 copy-start.3
  24.9 0.5 shard_map.55
  25.4 0.0 all-to-all-done
  25.4 0.0 copy-start.4
  25.4 0.2 copy-done.2
  25.6 0.0 copy-done.3
  25.6 0.4 copy-done.4
  26.1 3.5 %shard_map.57 = f32[64,8,128]{2,1,0:T(8,128)S(1)} custom-call(s32[12,256]{1,0:T(8,128)S(1)} %bitcast.14, s32[12,256]{1,0:T(8,128)S(1)} %bitcast.15, s32[1,256]{1,0:T(1,128)S(1)} %bitcast.16, bf16[640,256]{1,0:T(8,128)(2,1)S(1)} %get-tuple-element.7.refs_3_, f32[640,128]{1,0:T(8,128)S(1)} %get-tuple-element.8.refs_4_, bf16[256,128]{1,0:T(8,128)(2,1)S(1)} %bitcast.12), custom_call_target="tpu_custom_call" | custom-call | tf_op jit(solution)/shard_map/pallas_call | solution.py:175
  29.5 19.5 %all_to_all.10 = f32[32,2,8,128]{3,2,1,0:T(8,128)S(1)} all-to-all(f32[32,2,8,128]{3,2,1,0:T(8,128)S(1)} %bitcast.11), channel_id=1, replica_groups=mesh['tm'=16,'chan'=32] {'chan'}, dimensions={0} | all-to-all | bytes 524288 | tf_op jit(solution)/shard_map/all_to_all | solution.py:187
  49.0 0.8 %copy.8 = f32[8,8,8,128]{3,1,2,0:T(8,128)} copy(f32[8,8,8,128]{3,2,1,0:T(8,128)S(1)} %bitcast.17) | data formatting | bytes 524288
  (2 shorter events, 0.0 us)
Async XLA Ops:
  0.0 0.8 %copy-start.1 = (bf16[8,12,16]{2,0,1:T(8,128)(2,1)S(1)}, bf16[8,12,16]{2,0,1:T(8,128)(2,1)}, u32[]{:S(2)}) copy-start(bf16[8,12,16]{2,0,1:T(8,128)(2,1)} %param.6) | copy-start | bytes 9220
  0.7 9.8 %collective-permute-start = (bf16[24,512]{1,0:T(8,128)(2,1)S(1)}, bf16[24,512]{1,0:T(8,128)(2,1)S(1)}, u32[]{:S(2)}, u32[]{:S(2)}) collective-permute-start(bf16[24,512]{1,0:T(8,128)(2,1)S(1)} %slice.9), channel_id=1, source_target_pairs={{0,480},{32,0},{64,32},{96,64},{128,96},{160,128},{192,160},{224,1... | collective-permute-start | bytes 73736 | tf_op jit(solution)/shard_map/ppermute | solution.py:134
  1.5 23.9 %all-to-all-start = ((bf16[16,16,128]{2,1,0:T(8,128)(2,1)}), bf16[16,16,128]{2,1,0:T(8,128)(2,1)S(1)}, u32[]{:S(2)}, u32[]{:S(2)}) async-start(bf16[16,16,128]{2,1,0:T(8,128)(2,1)} %shard_map.56), calls=%async_computation | async-start | bytes 131072 | tf_op jit(solution)/shard_map/all_to_all | solution.py:138
  10.6 0.8 %slice-start = ((bf16[24,1024]{1,0:T(8,128)(2,1)}), bf16[16,1024]{1,0:T(8,128)(2,1)S(1)}, s32[]{:S(2)}) async-start(bf16[24,1024]{1,0:T(8,128)(2,1)} %rec.1), calls=%async_computation.2 | async-start | bytes 65536 | tf_op jit(solution)/shard_map/slice | solution.py:157
  11.3 13.6 %copy-start = (bf16[24,1024]{1,0:T(8,128)(2,1)S(1)}, bf16[24,1024]{1,0:T(8,128)(2,1)}, u32[]{:S(2)}) copy-start(bf16[24,1024]{1,0:T(8,128)(2,1)} %rec.1) | copy-start | bytes 147460
  11.3 13.6 %collective-permute-start.1 = (bf16[16,1536]{1,0:T(8,128)(2,1)S(1)}, bf16[16,1536]{1,0:T(8,128)(2,1)S(1)}, u32[]{:S(2)}, u32[]{:S(2)}) collective-permute-start(bf16[16,1536]{1,0:T(8,128)(2,1)S(1)} %pad_maximum_fusion), channel_id=1, source_target_pairs={{0,31},{1,0},{2,1},{3,2},{4,3},{5,4},{6,5},{7,6},{8,7},{9,8},{10,9... | collective-permute-start | bytes 147464 | tf_op jit(solution)/shard_map/ppermute | solution.py:134
  24.9 0.7 %copy-start.2 = (s32[256,12]{0,1:T(8,128)S(1)}, s32[256,12]{0,1:T(8,128)}, u32[]{:S(2)}) copy-start(s32[256,12]{0,1:T(8,128)} %param.7) | copy-start | bytes 36868
  24.9 0.7 %copy-start.3 = (s32[256,12]{0,1:T(8,128)S(1)}, s32[256,12]{0,1:T(8,128)}, u32[]{:S(2)}) copy-start(s32[256,12]{0,1:T(8,128)} %param.8) | copy-start | bytes 36868
  25.4 0.7 %copy-start.4 = (s32[256,1]{0,1:T(1,128)S(1)}, s32[256,1]{0,1:T(1,128)}, u32[]{:S(2)}) copy-start(s32[256,1]{0,1:T(1,128)} %param.9) | copy-start | bytes 3076

commit v3 on v2

--- a/solution.py
+++ b/solution.py
@@ -64,7 +64,7 @@
     ee[...] = both[:, :LANES] + pr[pl.ds(1, ALL_ROWS), :]
 
 
-def stack_kernel(total_chan, lists, moves, owners, xx, ee, waves, out, wr, we, sh):
+def stack_kernel(total_chan, table, xx, ee, waves, out, wr, we, sh):
     group = lax.axis_index("chan")
     wave_t = waves[...].astype(F32).T
     sample_id = lax.broadcasted_iota(jnp.int32, (L, L), 0)
@@ -91,16 +91,15 @@
 
     def one_template(k, carry):
         total = jnp.zeros((TPL, LANES), F32)
-        tpl = group * TPL + k
         for j in range(SLOTS):
             p = j * TPL + k
-            listed = lists[j, tpl]
+            listed = table[k, j]
             valid = listed >= 0
             place = listed - group * CH
             place = jnp.where(place < 0, place + total_chan, place)
             place = jnp.where(valid, place, 0)
             start = pl.multiple_of(place * ROWS, ROWS)
-            shift = moves[j, tpl]
+            shift = table[k, SLOTS + j]
             lanes, rows = shift & (LANES - 1), shift >> 7
             first, second = circulant(p, 0), circulant(p, 1)
             band = jnp.concatenate(
@@ -119,10 +118,10 @@
             after = sh[j, pl.ds(rows + 1, TPL), :]
             moved = jnp.where(lane_row < LANES - lanes, here, after)
             total = total + jnp.where(valid, moved, 0.0)
-        owner = owners[0, tpl]
+        owner = table[k, 2 * SLOTS]
         rank = jnp.int32(0)
         for q in range(TPL):
-            same = (owners[0, group * TPL + q] == owner) & (q < k)
+            same = (table[q, 2 * SLOTS] == owner) & (q < k)
             rank = rank + jnp.where(same, 1, 0)
         out[owner * SCAP + rank] = total
         return carry
@@ -157,6 +156,8 @@
     edge = jnp.concatenate([records[:SPILL], right[:SPILL]], axis=1)
     below = shifted(edge, "chan", n_chan)
     waves = gathered(chunks)
+    table = jnp.concatenate([channel_lists, moveouts, owner_map], axis=1)
+    table = lax.dynamic_slice_in_dim(table, lax.axis_index("chan") * TPL, TPL, 0)
     frames, energy = pl.pallas_call(
         frame_kernel,
         out_shape=(
@@ -175,7 +176,7 @@
     outgoing = pl.pallas_call(
         lambda *refs: stack_kernel(ch_dev * n_chan, *refs),
         out_shape=jax.ShapeDtypeStruct((n_chan * SCAP, TPL, LANES), F32),
-        in_specs=[smem] * 3 + [vmem] * 3,
+        in_specs=[smem] + [vmem] * 3,
         out_specs=vmem,
         scratch_shapes=[
             pltpu.VMEM((2, LANES, LANES), F32),
@@ -183,7 +184,7 @@
             pltpu.VMEM((SLOTS, ROWS, LANES), F32),
         ],
         compiler_params=params,
-    )(channel_lists.T, moveouts.T, owner_map.T, frames, energy, waves)
+    )(table, frames, energy, waves)
     incoming = lax.all_to_all(outgoing.reshape(n_chan, SCAP, TPL, LANES), "chan", 0, 0)
     return incoming.reshape(n_chan * SCAP, t_dev)
 

time: 50.2 us -> 49 us (0.976)
  local copies, waits for them, and re-layouts: 2.92 us -> 2.33 us
    unnamed x11 -> x12, local copies, waits for them, and re-layouts: 1.44 us -> 0.85 us
where the time goes in v3:
time: 49 us; the launch traced here: 48.6 us
  starting transfers between devices  21 us (43%)
  blocking collectives  19.5 us (40%)
  Pallas kernels  4.15 us (8%)
  local copies, waits for them, and re-layouts  2.33 us (5%)
  waiting for transfers between devices  1.55 us (3%)
    all_to_all x1, blocking collectives, local(): lax.all_to_all(outgoing.reshape(n_chan, SCAP, TPL, LANES), 'chan', 0, 0)  19.5 us
    ppermute x2, starting transfers between devices, shifted(): lax.ppermute(value, axis, [(s, (s - 1) % count) for s in range(count)])  11.8 us
    all_to_all x1, starting transfers between devices, gathered(): return lax.all_to_all(chunks, 'tm', 0, 0).reshape(L, LANES)  9.12 us
    pallas_call x1, Pallas kernels, local(): pl.pallas_call(lambda *refs: stack_kernel(ch_dev * n_chan, *refs), out_sh...  2.97 us
    ppermute x2, waiting for transfers between devices, shifted(): lax.ppermute(value, axis, [(s, (s - 1) % count) for s in range(count)])  1.54 us
  transfers between devices with their start and end apart: 3, of which 1 were waited for; matrix products, arithmetic and copies ran while one was open for 0% of the time, Pallas kernels for 2%

profile of v3, /device:TPU:8, one launch (start us, length us, event | category | flops | bytes accessed | tf_op | source)
XLA Modules:
  0.0 48.6 jit_solution(3716047378533240836)
XLA Ops:
  0.0 0.0 copy-start.1
  0.0 0.7 %slice.9 = bf16[24,512]{1,0:T(8,128)(2,1)S(1)} slice(bf16[24,1024]{1,0:T(8,128)(2,1)} %rec.1), slice={[0:24], [0:512]} | slice | bytes 49152 | tf_op jit(solution)/shard_map/slice | solution.py:155
  0.7 0.0 collective-permute-start
  0.8 0.0 copy-done.1
  0.8 0.7 %shard_map.56 = bf16[16,16,128]{2,1,0:T(8,128)(2,1)} custom-call(bf16[12,8,16]{2,1,0:T(8,128)(2,1)S(1)} %bitcast.10), custom_call_target="tpu_custom_call" | custom-call | tf_op jit(solution)/shard_map/pallas_call | solution.py:148
  1.5 9.1 %all-to-all-start = ((bf16[16,16,128]{2,1,0:T(8,128)(2,1)}), bf16[16,16,128]{2,1,0:T(8,128)(2,1)S(1)}, u32[]{:S(2)}, u32[]{:S(2)}) async-start(bf16[16,16,128]{2,1,0:T(8,128)(2,1)} %shard_map.56), calls=%async_computation | async-start | bytes 131072 | tf_op jit(solution)/shard_map/all_to_all | solution.py:137
  10.6 0.0 slice-start
  10.6 0.0 collective-permute-done.right
  10.6 0.7 %slice-done = bf16[16,1024]{1,0:T(8,128)(2,1)S(1)} async-done(((bf16[24,1024]{1,0:T(8,128)(2,1)}), bf16[16,1024]{1,0:T(8,128)(2,1)S(1)}, s32[]{:S(2)}) %slice-start) | async-done | bytes 32792 | tf_op jit(solution)/shard_map/slice | solution.py:156
  11.3 0.0 copy-start.2
  11.3 0.0 copy-start.3
  11.3 0.0 copy-start.4
  11.4 0.0 copy-start
  11.4 11.8 %collective-permute-start.1 = (bf16[16,1536]{1,0:T(8,128)(2,1)S(1)}, bf16[16,1536]{1,0:T(8,128)(2,1)S(1)}, u32[]{:S(2)}, u32[]{:S(2)}) collective-permute-start(bf16[16,1536]{1,0:T(8,128)(2,1)S(1)} %pad_maximum_fusion), channel_id=1, source_target_pairs={{0,31},{1,0},{2,1},{3,2},{4,3},{5,4},{6,5},{7,6},{8,7},{9,8},{10,9... | collective-permute-start | bytes 147464 | tf_op jit(solution)/shard_map/ppermute | solution.py:133
  23.2 0.0 copy-done.2
  23.2 0.0 copy-done.3
  23.2 0.0 copy-done.4
  23.2 0.1 fusion.1
  23.3 0.1 copy.10.refs_0_
  23.4 1.5 %collective-permute-done.1.below = bf16[16,1536]{1,0:T(8,128)(2,1)S(1)} collective-permute-done((bf16[16,1536]{1,0:T(8,128)(2,1)S(1)}, bf16[16,1536]{1,0:T(8,128)(2,1)S(1)}, u32[]{:S(2)}, u32[]{:S(2)}) %collective-permute-start.1) | collective-permute-done | bytes 49184 | tf_op jit(solution)/shard_map/ppermute | solution.py:133
  24.9 0.0 copy-done
  24.9 0.5 shard_map.55
  25.4 0.0 all-to-all-done
  25.4 3.0 %shard_map.57 = f32[64,8,128]{2,1,0:T(8,128)S(1)} custom-call(s32[8,25]{1,0:T(8,128)S(1)} %copy.10.refs_0_, bf16[640,256]{1,0:T(8,128)(2,1)S(1)} %get-tuple-element.7.refs_1_, f32[640,128]{1,0:T(8,128)S(1)} %get-tuple-element.8.refs_2_, bf16[256,128]{1,0:T(8,128)(2,1)S(1)} %bitcast.9), custom_call_target="tpu_custom_call" | custom-call | tf_op jit(solution)/shard_map/pallas_call | solution.py:176
  28.4 19.5 %all_to_all.10 = f32[32,2,8,128]{3,2,1,0:T(8,128)S(1)} all-to-all(f32[32,2,8,128]{3,2,1,0:T(8,128)S(1)} %bitcast.8), channel_id=1, replica_groups=mesh['tm'=16,'chan'=32] {'chan'}, dimensions={0} | all-to-all | bytes 524288 | tf_op jit(solution)/shard_map/all_to_all | solution.py:188
  47.9 0.8 %copy.13 = f32[8,8,8,128]{3,1,2,0:T(8,128)} copy(f32[8,8,8,128]{3,2,1,0:T(8,128)S(1)} %bitcast.11) | data formatting | bytes 524288
  (2 shorter events, 0.0 us)
Async XLA Ops:
  0.0 0.8 %copy-start.1 = (bf16[8,12,16]{2,0,1:T(8,128)(2,1)S(1)}, bf16[8,12,16]{2,0,1:T(8,128)(2,1)}, u32[]{:S(2)}) copy-start(bf16[8,12,16]{2,0,1:T(8,128)(2,1)} %param.6) | copy-start | bytes 9220
  0.7 9.8 %collective-permute-start = (bf16[24,512]{1,0:T(8,128)(2,1)S(1)}, bf16[24,512]{1,0:T(8,128)(2,1)S(1)}, u32[]{:S(2)}, u32[]{:S(2)}) collective-permute-start(bf16[24,512]{1,0:T(8,128)(2,1)S(1)} %slice.9), channel_id=1, source_target_pairs={{0,480},{32,0},{64,32},{96,64},{128,96},{160,128},{192,160},{224,1... | collective-permute-start | bytes 73736 | tf_op jit(solution)/shard_map/ppermute | solution.py:133
  1.5 24.0 %all-to-all-start = ((bf16[16,16,128]{2,1,0:T(8,128)(2,1)}), bf16[16,16,128]{2,1,0:T(8,128)(2,1)S(1)}, u32[]{:S(2)}, u32[]{:S(2)}) async-start(bf16[16,16,128]{2,1,0:T(8,128)(2,1)} %shard_map.56), calls=%async_computation | async-start | bytes 131072 | tf_op jit(solution)/shard_map/all_to_all | solution.py:137
  10.6 0.8 %slice-start = ((bf16[24,1024]{1,0:T(8,128)(2,1)}), bf16[16,1024]{1,0:T(8,128)(2,1)S(1)}, s32[]{:S(2)}) async-start(bf16[24,1024]{1,0:T(8,128)(2,1)} %rec.1), calls=%async_computation.2 | async-start | bytes 65536 | tf_op jit(solution)/shard_map/slice | solution.py:156
  11.3 11.9 %copy-start.2 = (s32[256,12]{0,1:T(8,128)S(1)}, s32[256,12]{0,1:T(8,128)}, u32[]{:S(2)}) copy-start(s32[256,12]{0,1:T(8,128)} %param.7) | copy-start | bytes 36868
  11.3 11.9 %copy-start.3 = (s32[256,12]{0,1:T(8,128)S(1)}, s32[256,12]{0,1:T(8,128)}, u32[]{:S(2)}) copy-start(s32[256,12]{0,1:T(8,128)} %param.8) | copy-start | bytes 36868
  11.3 11.9 %copy-start.4 = (s32[256,1]{0,1:T(1,128)S(1)}, s32[256,1]{0,1:T(1,128)}, u32[]{:S(2)}) copy-start(s32[256,1]{0,1:T(1,128)} %param.9) | copy-start | bytes 3076
  11.4 13.6 %copy-start = (bf16[24,1024]{1,0:T(8,128)(2,1)S(1)}, bf16[24,1024]{1,0:T(8,128)(2,1)}, u32[]{:S(2)}) copy-start(bf16[24,1024]{1,0:T(8,128)(2,1)} %rec.1) | copy-start | bytes 147460
  11.4 13.6 %collective-permute-start.1 = (bf16[16,1536]{1,0:T(8,128)(2,1)S(1)}, bf16[16,1536]{1,0:T(8,128)(2,1)S(1)}, u32[]{:S(2)}, u32[]{:S(2)}) collective-permute-start(bf16[16,1536]{1,0:T(8,128)(2,1)S(1)} %pad_maximum_fusion), channel_id=1, source_target_pairs={{0,31},{1,0},{2,1},{3,2},{4,3},{5,4},{6,5},{7,6},{8,7},{9,8},{10,9... | collective-permute-start | bytes 147464 | tf_op jit(solution)/shard_map/ppermute | solution.py:133

commit v4 on v3

v4 whole, which is shorter than its diff:
```python
import jax
import jax.numpy as jnp
from jax import lax
from jax.experimental import pallas as pl
from jax.experimental.pallas import tpu as pltpu
from jax.sharding import PartitionSpec as P

L = 256
SLOTS = 12
SPILL = 16
LANES = 128
ROWS = 16
HALO = 512
TPL = 8
CH = 24
SCAP = 2
PAIRS = TPL * SLOTS
FROM = 16
F32 = jnp.float32
BF16 = jnp.bfloat16


def chunk_kernel(waves, out):
    rows = [waves[j].astype(F32) for j in range(SLOTS)]
    flat = jnp.concatenate(rows + [jnp.zeros((LANES - PAIRS, rows[0].shape[1]), F32)], axis=0)
    wide = jnp.concatenate([flat, jnp.zeros((LANES, LANES - flat.shape[1]), F32)], axis=1)
    turned = wide.T[: out.shape[1]]
    last = out.shape[1] - 1
    turned = jnp.concatenate([turned[last - i : last - i + 1] for i in range(last + 1)], axis=0).astype(BF16)
    for i in range(out.shape[0]):
        out[i] = turned


def triangles():
    row_id = lax.broadcasted_iota(jnp.int32, (LANES, LANES), 0)
    lane_id = lax.broadcasted_iota(jnp.int32, (LANES, LANES), 1)
    lower = jnp.where(row_id >= lane_id, 1.0, 0.0).astype(BF16)
    upper = jnp.where(row_id < lane_id, 1.0, 0.0).astype(BF16)
    return lower, upper


def frame_pairs(xs, pr, rows):
    tri = jnp.concatenate(triangles(), axis=1)
    ones_band = jnp.concatenate([tri, tri], axis=0)
    pair = jnp.concatenate([xs[pl.ds(0, rows), :], xs[pl.ds(1, rows), :]], axis=1)
    square = pair * pair
    high = square.astype(BF16)
    low = (square - high.astype(F32)).astype(BF16)
    both = jnp.dot(high, ones_band, preferred_element_type=F32) + jnp.dot(
        low, ones_band, preferred_element_type=F32
    )
    pr[pl.ds(0, rows), :] = both[:, LANES:]
    pr[pl.ds(rows, 8), :] = jnp.zeros((8, LANES), F32)
    return pair.astype(BF16), both[:, :LANES] + pr[pl.ds(1, rows), :]


def frame_kernel(rec, right, xx, ee, xs, pr):
    for b in range(12):
        part, at = (rec, b) if b < 8 else (right, b - 8)
        xs[pl.ds(b, CH, stride=ROWS), :] = part[:, LANES * at : LANES * (at + 1)].astype(F32)
    for b in range(12, ROWS):
        xs[pl.ds(b, CH, stride=ROWS), :] = jnp.zeros((CH, LANES), F32)
    xs[pl.ds(CH * ROWS, 8), :] = jnp.zeros((8, LANES), F32)
    xx[...], ee[...] = frame_pairs(xs, pr, CH * ROWS)


def own_slots(k):
    return min(SLOTS, max(0, CH - 5 - 3 * k))


def stacked(table, k, slots, first_row, total_chan, xx, ee, wr, we, sh):
    group = lax.axis_index("chan")
    lower, upper = triangles()
    lane_row = lax.broadcasted_iota(jnp.int32, (TPL, LANES), 1)

    def circulant(p, half):
        row = wr[half, pl.ds(p, 1), :]
        full = jnp.broadcast_to(row, (LANES, LANES)).astype(BF16)
        return pltpu.roll(full, 1, 1, stride=1, stride_axis=0)

    total = jnp.zeros((TPL, LANES), F32)
    for j in slots:
        p = j * TPL + k
        listed = table[k, j]
        valid = listed >= 0
        place = listed - group * CH
        place = jnp.where(place < 0, place + total_chan, place) - first_row
        place = jnp.where(valid, place, 0)
        start = pl.multiple_of(place * ROWS, ROWS)
        shift = table[k, SLOTS + j]
        lanes, rows = shift & (LANES - 1), shift >> 7
        first, second = circulant(p, 0), circulant(p, 1)
        band = jnp.concatenate(
            [
                jnp.concatenate([first * lower, first * upper], axis=1),
                jnp.concatenate([second * lower, second * upper], axis=1),
            ],
            axis=0,
        )
        prod = jnp.dot(xx[pl.ds(start, ROWS), :], band, preferred_element_type=F32)
        corr = prod[:, :LANES] + pltpu.roll(prod[:, LANES:], ROWS - 1, 0)
        scale = we[pl.ds(p, 1), :] * ee[pl.ds(start, ROWS), :] + 1e-06
        normed = corr * lax.rsqrt(scale)
        sh[j] = pltpu.roll(normed, (LANES - lanes) & (LANES - 1), 1)
        here = sh[j, pl.ds(rows, TPL), :]
        after = sh[j, pl.ds(rows + 1, TPL), :]
        moved = jnp.where(lane_row < LANES - lanes, here, after)
        total = total + jnp.where(valid, moved, 0.0)
    return total


def own_kernel(total_chan, table_v, xx, ee, waves, part, wr, we, sh, table, sem):
    copy = pltpu.make_async_copy(table_v, table, sem)
    copy.start()
    order = [h + i for h in (0, LANES) for i in reversed(range(0, LANES, ROWS))]
    wave_t = jnp.concatenate([waves[pl.ds(i, ROWS), :].astype(F32) for i in order], axis=0).T
    wr[0] = wave_t[:, :LANES]
    wr[1] = wave_t[:, LANES:]
    we[...] = jnp.broadcast_to(jnp.sum(wave_t * wave_t, axis=1, keepdims=True), we.shape)
    copy.wait()
    for k in range(TPL):
        part[k] = stacked(table, k, range(own_slots(k)), 0, total_chan, xx, ee, wr, we, sh)


def rest_kernel(total_chan, table_v, own_xx, own_ee, below, part, wr, we, out, xs, pr, xx, ee, sh, table, sem):
    copy = pltpu.make_async_copy(table_v, table, sem)
    copy.start()
    for b in range(12):
        xs[pl.ds(b, SPILL, stride=ROWS), :] = below[:, LANES * b : LANES * (b + 1)].astype(F32)
    for b in range(12, ROWS):
        xs[pl.ds(b, SPILL, stride=ROWS), :] = jnp.zeros((SPILL, LANES), F32)
    xs[pl.ds(SPILL * ROWS, 8), :] = jnp.zeros((8, LANES), F32)
    kept = (CH - FROM) * ROWS
    xx[pl.ds(0, kept), :] = own_xx[pl.ds(FROM * ROWS, kept), :]
    ee[pl.ds(0, kept), :] = own_ee[pl.ds(FROM * ROWS, kept), :]
    pairs, energy = frame_pairs(xs, pr, SPILL * ROWS)
    xx[pl.ds(kept, SPILL * ROWS), :] = pairs
    ee[pl.ds(kept, SPILL * ROWS), :] = energy

    out[...] = jnp.zeros_like(out)
    copy.wait()
    for k in range(TPL):
        slots = range(own_slots(k), SLOTS)
        total = part[k] + stacked(table, k, slots, FROM, total_chan, xx, ee, wr, we, sh)
        owner = table[k, 2 * SLOTS]
        rank = jnp.int32(0)
        for q in range(k):
            rank = rank + jnp.where(table[q, 2 * SLOTS] == owner, 1, 0)
        out[owner * SCAP + rank] = total


def shifted(value, axis, count):
    return lax.ppermute(value, axis, [(s, (s - 1) % count) for s in range(count)])


def gathered(chunks):
    return lax.all_to_all(chunks, "tm", 0, 0).reshape(L, LANES)


def local(records, template_waves, channel_lists, moveouts, owner_map):
    ch_dev, t_dev = records.shape
    n_chan = lax.axis_size("chan")
    n_tm = lax.axis_size("tm")
    vmem = pl.BlockSpec(memory_space=pltpu.VMEM)
    params = pltpu.CompilerParams(vmem_limit_bytes=24 * 1024 * 1024)

    chunks = pl.pallas_call(
        chunk_kernel,
        out_shape=jax.ShapeDtypeStruct((n_tm, L // n_tm, LANES), BF16),
        in_specs=[vmem],
        out_specs=vmem,
        compiler_params=params,
    )(jnp.transpose(template_waves, (1, 0, 2)))
    right = shifted(records, "tm", n_tm)
    edge = jnp.concatenate([records[:SPILL], right[:SPILL, :HALO]], axis=1)
    lists, shifts, owners, edge = lax.optimization_barrier((channel_lists, moveouts, owner_map, edge))
    below = shifted(edge, "chan", n_chan)
    table = jnp.concatenate([lists, shifts, owners], axis=1)
    table = lax.dynamic_slice_in_dim(table, lax.axis_index("chan") * TPL, TPL, 0)
    waves = gathered(chunks)
    scalars = [pltpu.SMEM((TPL, 2 * SLOTS + 1), jnp.int32), pltpu.SemaphoreType.DMA]

    def scratch(*shape):
        return pltpu.VMEM(shape, F32)

    frames, energy = pl.pallas_call(
        frame_kernel,
        out_shape=(
            jax.ShapeDtypeStruct((CH * ROWS, 2 * LANES), BF16),
            jax.ShapeDtypeStruct((CH * ROWS, LANES), F32),
        ),
        in_specs=[vmem] * 2,
        out_specs=(vmem, vmem),
        scratch_shapes=[scratch(CH * ROWS + 8, LANES)] * 2,
        compiler_params=params,
        cost_estimate=pl.CostEstimate(flops=200_000_000, bytes_accessed=1_000_000, transcendentals=0),
    )(records, right)
    part, rows_w, energy_w = pl.pallas_call(
        lambda *refs: own_kernel(ch_dev * n_chan, *refs),
        out_shape=(
            jax.ShapeDtypeStruct((TPL, TPL, LANES), F32),
            jax.ShapeDtypeStruct((2, LANES, LANES), F32),
            jax.ShapeDtypeStruct((LANES, LANES), F32),
        ),
        in_specs=[vmem] * 4,
        out_specs=(vmem,) * 3,
        scratch_shapes=[scratch(SLOTS, ROWS, LANES)] + scalars,
        compiler_params=params,
        cost_estimate=pl.CostEstimate(flops=1_000_000_000, bytes_accessed=1_000_000, transcendentals=0),
    )(table, frames, energy, waves)
    late_rows = (CH - FROM + SPILL) * ROWS
    outgoing = pl.pallas_call(
        lambda *refs: rest_kernel(ch_dev * n_chan, *refs),
        out_shape=jax.ShapeDtypeStruct((n_chan * SCAP, TPL, LANES), F32),
        in_specs=[vmem] * 7,
        out_specs=vmem,
        scratch_shapes=[
            scratch(SPILL * ROWS + 8, LANES),
            scratch(SPILL * ROWS + 8, LANES),
            pltpu.VMEM((late_rows, 2 * LANES), BF16),
            scratch(late_rows, LANES),
            scratch(SLOTS, ROWS, LANES),
        ]
        + scalars,
        compiler_params=params,
    )(table, frames, energy, below, part, rows_w, energy_w)
    incoming = lax.all_to_all(outgoing.reshape(n_chan, SCAP, TPL, LANES), "chan", 0, 0)
    return incoming.reshape(n_chan * SCAP, t_dev)


def solution(mesh):
    in_specs = (P("chan", "tm"), P("chan", None, "tm"), P(), P(), P())
    out_specs = P("chan", "tm")
    return jax.shard_map(local, mesh=mesh, in_specs=in_specs, out_specs=out_specs, check_vma=False)
```

time: 49 us -> 47.4 us (0.967)
  waiting for transfers between devices: 1.55 us -> 0.01 us
  blocking collectives: 19.5 us -> 18.9 us
  Pallas kernels: 4.15 us -> 4.67 us
    ppermute x2, waiting for transfers between devices: 1.54 us -> 0.01 us  [shifted(): lax.ppermute(value, axis, [(s, (s - 1) % count) for s in range(count)])]
    slice x4 -> x2, local copies, waits for them, and re-layouts: 1.48 us -> 0.01 us  [local(): edge = jnp.concatenate([records[:SPILL], right[:SPILL, :HALO]], axis=1)]
    unnamed x12, local copies, waits for them, and re-layouts: 0.85 us -> 2.27 us
    all_to_all x1, blocking collectives: 19.5 us -> 18.9 us  [local(): lax.all_to_all(outgoing.reshape(n_chan, SCAP, TPL, LANES), 'chan', 0, 0)]
    pallas_call x2 -> x3, Pallas kernels: 3.44 us -> 3.96 us  [the longest x1 1.98 us: local(): pl.pallas_call(lambda *refs: own_kernel(ch_dev * n_chan, *refs), out_shap...]
  transfers between devices with their start and end apart: 3 -> 3, of which waited for: 1 -> 0; matrix products, arithmetic and copies ran while one was open for 0% -> 0% of each run, Pallas kernels for 2% -> 6%
where the time goes in v4:
time: 47.4 us; the launch traced here: 47 us
  starting transfers between devices  20.9 us (44%)
  blocking collectives  18.9 us (40%)
  Pallas kernels  4.67 us (10%)
  local copies, waits for them, and re-layouts  2.28 us (5%)
    all_to_all x1, blocking collectives, local(): lax.all_to_all(outgoing.reshape(n_chan, SCAP, TPL, LANES), 'chan', 0, 0)  18.9 us
    ppermute x2, starting transfers between devices, shifted(): lax.ppermute(value, axis, [(s, (s - 1) % count) for s in range(count)])  11.7 us
    all_to_all x1, starting transfers between devices, gathered(): return lax.all_to_all(chunks, 'tm', 0, 0).reshape(L, LANES)  9.25 us
    unnamed x12, local copies, waits for them, and re-layouts  2.27 us
    pallas_call x1, Pallas kernels, local(): pl.pallas_call(lambda *refs: own_kernel(ch_dev * n_chan, *refs), out_shap...  1.98 us
    pallas_call x1, Pallas kernels, local(): pl.pallas_call(lambda *refs: rest_kernel(ch_dev * n_chan, *refs), out_sha...  1.65 us
  transfers between devices with their start and end apart: 3, of which 0 were waited for; matrix products, arithmetic and copies ran while one was open for 0% of the time, Pallas kernels for 6%

profile of v4, /device:TPU:8, one launch (start us, length us, event | category | flops | bytes accessed | tf_op | source)
XLA Modules:
  0.0 47.0 jit_solution(2307293400205417505)
XLA Ops:
  0.0 0.0 collective-permute-start
  0.0 0.0 copy-start
  0.0 0.7 %copy-done = bf16[8,12,16]{2,0,1:T(8,128)(2,1)S(1)} copy-done((bf16[8,12,16]{2,0,1:T(8,128)(2,1)S(1)}, bf16[8,12,16]{2,0,1:T(8,128)(2,1)}, u32[]{:S(2)}) %copy-start) | copy-done | bytes 3096
  0.7 0.7 %shard_map.56 = bf16[16,16,128]{2,1,0:T(8,128)(2,1)} custom-call(bf16[12,8,16]{2,1,0:T(8,128)(2,1)S(1)} %bitcast.10), custom_call_target="tpu_custom_call" | custom-call | tf_op jit(solution)/shard_map/pallas_call | solution.py:167
  1.5 0.0 copy-start.1
  1.5 9.3 %all-to-all-start = ((bf16[16,16,128]{2,1,0:T(8,128)(2,1)}), bf16[16,16,128]{2,1,0:T(8,128)(2,1)S(1)}, u32[]{:S(2)}, u32[]{:S(2)}) async-start(bf16[16,16,128]{2,1,0:T(8,128)(2,1)} %shard_map.56), calls=%async_computation | async-start | bytes 131072 | tf_op jit(solution)/shard_map/all_to_all | solution.py:157
  10.7 0.0 copy-done.1
  10.7 0.0 collective-permute-done.right
  10.8 0.0 copy-start.2
  10.8 0.0 copy-start.3
  10.8 0.0 copy-start.4
  10.8 0.7 %copy-done.2 = s32[256,12]{0,1:T(8,128)S(1)} copy-done((s32[256,12]{0,1:T(8,128)S(1)}, s32[256,12]{0,1:T(8,128)}, u32[]{:S(2)}) %copy-start.2) | copy-done | bytes 12312
  11.5 0.0 copy-done.3
  11.5 0.0 copy-done.4
  11.5 0.1 fusion.1
  11.6 0.1 copy.10.refs_0_
  11.6 11.7 %collective-permute-start.1 = (bf16[16,1536]{1,0:T(8,128)(2,1)S(1)}, bf16[16,1536]{1,0:T(8,128)(2,1)S(1)}, u32[]{:S(2)}, u32[]{:S(2)}) collective-permute-start(bf16[16,1536]{1,0:T(8,128)(2,1)S(1)} %pad_maximum_fusion), channel_id=1, source_target_pairs={{0,31},{1,0},{2,1},{3,2},{4,3},{5,4},{6,5},{7,6},{8,7},{9,8},{10,9... | collective-permute-start | bytes 147464 | tf_op jit(solution)/shard_map/ppermute | solution.py:153
  23.3 0.3 shard_map.55
  23.7 0.0 all-to-all-done
  23.7 2.0 %shard_map.57 = (f32[8,8,128]{2,1,0:T(8,128)S(1)}, f32[2,128,128]{2,1,0:T(8,128)S(1)}, f32[128,128]{1,0:T(8,128)S(1)}) custom-call(s32[8,25]{1,0:T(8,128)S(1)} %copy.10.refs_0_, bf16[384,256]{1,0:T(8,128)(2,1)S(1)} %get-tuple-element.17.refs_1_, f32[384,128]{1,0:T(8,128)S(1)} %get-tuple-element.18.refs_2_, bf16[256,128]{1,0:T(8,128)(2,1)S(1)} %bitcast.9), custom_call_target="tpu_custom_call" | custom-call | flops 1000000000 | bytes 1000000 | tf_op jit(solution)/shard_map/pallas_call | solution.py:198
  25.7 0.0 collective-permute-done.1.refs_3_
  25.7 1.6 %shard_map.58 = f32[64,8,128]{2,1,0:T(8,128)S(1)} custom-call(s32[8,25]{1,0:T(8,128)S(1)} %copy.10.refs_0_, bf16[384,256]{1,0:T(8,128)(2,1)S(1)} %get-tuple-element.17.refs_1_, f32[384,128]{1,0:T(8,128)S(1)} %get-tuple-element.18.refs_2_, bf16[16,1536]{1,0:T(8,128)(2,1)S(1)} %collective-permute-done.1.refs_3_, f32[8,8,128]{2,1,0:T(8,128)S(1)} %get-tuple-element.20.refs_4_, ...), custom_call_target="tpu_custom_call" | custom-call | tf_op jit(solution)/shard_map/pallas_call | solution.py:212
  27.3 18.9 %all_to_all.10 = f32[32,2,8,128]{3,2,1,0:T(8,128)S(1)} all-to-all(f32[32,2,8,128]{3,2,1,0:T(8,128)S(1)} %bitcast.8), channel_id=1, replica_groups=mesh['tm'=16,'chan'=32] {'chan'}, dimensions={0} | all-to-all | bytes 524288 | tf_op jit(solution)/shard_map/all_to_all | solution.py:227
  46.2 0.8 %copy.13 = f32[8,8,8,128]{3,1,2,0:T(8,128)} copy(f32[8,8,8,128]{3,2,1,0:T(8,128)S(1)} %bitcast.11) | data formatting | bytes 524288
  (3 shorter events, 0.0 us)
Async XLA Ops:
  0.0 10.7 %collective-permute-start = (bf16[24,1024]{1,0:T(8,128)(2,1)}, bf16[24,1024]{1,0:T(8,128)(2,1)S(1)}, u32[]{:S(2)}, u32[]{:S(2)}) collective-permute-start(bf16[24,1024]{1,0:T(8,128)(2,1)} %rec.1), channel_id=1, source_target_pairs={{0,480},{32,0},{64,32},{96,64},{128,96},{160,128},{192,160},{224,1... | collective-permute-start | bytes 147464 | tf_op jit(solution)/shard_map/ppermute | solution.py:153
  0.0 0.7 %copy-start = (bf16[8,12,16]{2,0,1:T(8,128)(2,1)S(1)}, bf16[8,12,16]{2,0,1:T(8,128)(2,1)}, u32[]{:S(2)}) copy-start(bf16[8,12,16]{2,0,1:T(8,128)(2,1)} %param.6) | copy-start | bytes 9220
  1.5 9.3 %copy-start.1 = (bf16[24,1024]{1,0:T(8,128)(2,1)S(1)}, bf16[24,1024]{1,0:T(8,128)(2,1)}, u32[]{:S(2)}) copy-start(bf16[24,1024]{1,0:T(8,128)(2,1)} %rec.1) | copy-start | bytes 147460
  1.5 22.2 %all-to-all-start = ((bf16[16,16,128]{2,1,0:T(8,128)(2,1)}), bf16[16,16,128]{2,1,0:T(8,128)(2,1)S(1)}, u32[]{:S(2)}, u32[]{:S(2)}) async-start(bf16[16,16,128]{2,1,0:T(8,128)(2,1)} %shard_map.56), calls=%async_computation | async-start | bytes 131072 | tf_op jit(solution)/shard_map/all_to_all | solution.py:157
  10.8 0.7 %copy-start.2 = (s32[256,12]{0,1:T(8,128)S(1)}, s32[256,12]{0,1:T(8,128)}, u32[]{:S(2)}) copy-start(s32[256,12]{0,1:T(8,128)} %param.7) | copy-start | bytes 36868
  10.8 0.7 %copy-start.3 = (s32[256,12]{0,1:T(8,128)S(1)}, s32[256,12]{0,1:T(8,128)}, u32[]{:S(2)}) copy-start(s32[256,12]{0,1:T(8,128)} %param.8) | copy-start | bytes 36868
  10.8 0.7 %copy-start.4 = (s32[256,1]{0,1:T(1,128)S(1)}, s32[256,1]{0,1:T(1,128)}, u32[]{:S(2)}) copy-start(s32[256,1]{0,1:T(1,128)} %param.9) | copy-start | bytes 3076
  11.6 14.0 %collective-permute-start.1 = (bf16[16,1536]{1,0:T(8,128)(2,1)S(1)}, bf16[16,1536]{1,0:T(8,128)(2,1)S(1)}, u32[]{:S(2)}, u32[]{:S(2)}) collective-permute-start(bf16[16,1536]{1,0:T(8,128)(2,1)S(1)} %pad_maximum_fusion), channel_id=1, source_target_pairs={{0,31},{1,0},{2,1},{3,2},{4,3},{5,4},{6,5},{7,6},{8,7},{9,8},{10,9... | collective-permute-start | bytes 147464 | tf_op jit(solution)/shard_map/ppermute | solution.py:153

commit v5 on v4

--- a/solution.py
+++ b/solution.py
@@ -146,7 +146,7 @@
         rank = jnp.int32(0)
         for q in range(k):
             rank = rank + jnp.where(table[q, 2 * SLOTS] == owner, 1, 0)
-        out[owner * SCAP + rank] = total
+        out[(out.shape[0] // SCAP - 1 - owner) * SCAP + rank] = total
 
 
 def shifted(value, axis, count):
@@ -224,7 +224,13 @@
         + scalars,
         compiler_params=params,
     )(table, frames, energy, below, part, rows_w, energy_w)
-    incoming = lax.all_to_all(outgoing.reshape(n_chan, SCAP, TPL, LANES), "chan", 0, 0)
+    incoming = lax.all_to_all(
+        outgoing.reshape(n_chan, SCAP, TPL, LANES),
+        "chan",
+        0,
+        0,
+        axis_index_groups=[list(reversed(range(n_chan)))],
+    )[::-1]
     return incoming.reshape(n_chan * SCAP, t_dev)
 
 

time: 47.4 us -> 44.6 us (0.941)
  the two profiles are of different devices: /device:TPU:8 before, /device:TPU:6 now
where the time goes in v5:
time: 44.6 us; the launch traced here: 44.2 us
  blocking collectives  23 us (52%)
  starting transfers between devices  10.2 us (23%)
  Pallas kernels  4.66 us (10%)
  waiting for transfers between devices  3.85 us (9%)
  local copies, waits for them, and re-layouts  2.3 us (5%)
    all_to_all x1, blocking collectives, local(): lax.all_to_all(outgoing.reshape(n_chan, SCAP, TPL, LANES), 'chan', 0, 0,...  23 us
    ppermute x2, starting transfers between devices, shifted(): lax.ppermute(value, axis, [(s, (s - 1) % count) for s in range(count)])  5.64 us
    all_to_all x1, starting transfers between devices, gathered(): return lax.all_to_all(chunks, 'tm', 0, 0).reshape(L, LANES)  4.54 us
    all_to_all x1, waiting for transfers between devices, gathered(): return lax.all_to_all(chunks, 'tm', 0, 0).reshape(L, LANES)  3.85 us
    unnamed x12, local copies, waits for them, and re-layouts  2.27 us
    pallas_call x1, Pallas kernels, local(): pl.pallas_call(lambda *refs: own_kernel(ch_dev * n_chan, *refs), out_shap...  1.97 us
    pallas_call x1, Pallas kernels, local(): pl.pallas_call(lambda *refs: rest_kernel(ch_dev * n_chan, *refs), out_sha...  1.64 us
  transfers between devices with their start and end apart: 3, of which 1 were waited for; matrix products, arithmetic and copies ran while one was open for 0% of the time, Pallas kernels for 7%

profile of v5, /device:TPU:6, one launch (start us, length us, event | category | flops | bytes accessed | tf_op | source)
XLA Modules:
  0.0 44.2 jit_solution(15125668418912015209)
XLA Ops:
  0.0 2.9 %collective-permute-start = (bf16[24,1024]{1,0:T(8,128)(2,1)}, bf16[24,1024]{1,0:T(8,128)(2,1)S(1)}, u32[]{:S(2)}, u32[]{:S(2)}) collective-permute-start(bf16[24,1024]{1,0:T(8,128)(2,1)} %rec.1), channel_id=1, source_target_pairs={{0,480},{32,0},{64,32},{96,64},{128,96},{160,128},{192,160},{224,1... | collective-permute-start | bytes 147464 | tf_op jit(solution)/shard_map/ppermute | solution.py:153
  2.9 0.0 copy-start
  2.9 0.7 %copy-done = bf16[8,12,16]{2,0,1:T(8,128)(2,1)S(1)} copy-done((bf16[8,12,16]{2,0,1:T(8,128)(2,1)S(1)}, bf16[8,12,16]{2,0,1:T(8,128)(2,1)}, u32[]{:S(2)}) %copy-start) | copy-done | bytes 3096
  3.6 0.7 %shard_map.56 = bf16[16,16,128]{2,1,0:T(8,128)(2,1)} custom-call(bf16[12,8,16]{2,1,0:T(8,128)(2,1)S(1)} %bitcast.10), custom_call_target="tpu_custom_call" | custom-call | tf_op jit(solution)/shard_map/pallas_call | solution.py:167
  4.4 0.0 copy-start.1
  4.4 4.5 %all-to-all-start = ((bf16[16,16,128]{2,1,0:T(8,128)(2,1)}), bf16[16,16,128]{2,1,0:T(8,128)(2,1)S(1)}, u32[]{:S(2)}, u32[]{:S(2)}) async-start(bf16[16,16,128]{2,1,0:T(8,128)(2,1)} %shard_map.56), calls=%async_computation | async-start | bytes 131072 | tf_op jit(solution)/shard_map/all_to_all | solution.py:157
  8.9 0.0 copy-done.1
  8.9 0.0 collective-permute-done.right
  9.0 0.0 copy-start.2
  9.0 0.0 copy-start.3
  9.0 0.0 copy-start.4
  9.0 0.7 %copy-done.2 = s32[256,12]{0,1:T(8,128)S(1)} copy-done((s32[256,12]{0,1:T(8,128)S(1)}, s32[256,12]{0,1:T(8,128)}, u32[]{:S(2)}) %copy-start.2) | copy-done | bytes 12312
  9.7 0.0 copy-done.3
  9.7 0.0 copy-done.4
  9.7 0.1 fusion.1
  9.8 0.1 copy.10.refs_0_
  9.9 2.7 %collective-permute-start.1 = (bf16[16,1536]{1,0:T(8,128)(2,1)S(1)}, bf16[16,1536]{1,0:T(8,128)(2,1)S(1)}, u32[]{:S(2)}, u32[]{:S(2)}) collective-permute-start(bf16[16,1536]{1,0:T(8,128)(2,1)S(1)} %pad_maximum_fusion), channel_id=1, source_target_pairs={{0,31},{1,0},{2,1},{3,2},{4,3},{5,4},{6,5},{7,6},{8,7},{9,8},{10,9... | collective-permute-start | bytes 147464 | tf_op jit(solution)/shard_map/ppermute | solution.py:153
  12.6 0.3 shard_map.55
  12.9 3.8 %all-to-all-done = bf16[16,16,128]{2,1,0:T(8,128)(2,1)S(1)} async-done(((bf16[16,16,128]{2,1,0:T(8,128)(2,1)}), bf16[16,16,128]{2,1,0:T(8,128)(2,1)S(1)}, u32[]{:S(2)}, u32[]{:S(2)}) %all-to-all-start) | async-done | bytes 65568 | tf_op jit(solution)/shard_map/all_to_all | solution.py:157
  16.8 2.0 %shard_map.57 = (f32[8,8,128]{2,1,0:T(8,128)S(1)}, f32[2,128,128]{2,1,0:T(8,128)S(1)}, f32[128,128]{1,0:T(8,128)S(1)}) custom-call(s32[8,25]{1,0:T(8,128)S(1)} %copy.10.refs_0_, bf16[384,256]{1,0:T(8,128)(2,1)S(1)} %get-tuple-element.17.refs_1_, f32[384,128]{1,0:T(8,128)S(1)} %get-tuple-element.18.refs_2_, bf16[256,128]{1,0:T(8,128)(2,1)S(1)} %bitcast.9), custom_call_target="tpu_custom_call" | custom-call | flops 1000000000 | bytes 1000000 | tf_op jit(solution)/shard_map/pallas_call | solution.py:198
  18.8 0.0 collective-permute-done.1.refs_3_
  18.8 1.6 %shard_map.58 = f32[64,8,128]{2,1,0:T(8,128)S(1)} custom-call(s32[8,25]{1,0:T(8,128)S(1)} %copy.10.refs_0_, bf16[384,256]{1,0:T(8,128)(2,1)S(1)} %get-tuple-element.17.refs_1_, f32[384,128]{1,0:T(8,128)S(1)} %get-tuple-element.18.refs_2_, bf16[16,1536]{1,0:T(8,128)(2,1)S(1)} %collective-permute-done.1.refs_3_, f32[8,8,128]{2,1,0:T(8,128)S(1)} %get-tuple-element.20.refs_4_, ...), custom_call_target="tpu_custom_call" | custom-call | tf_op jit(solution)/shard_map/pallas_call | solution.py:212
  20.4 23.0 %all_to_all.10 = f32[32,2,8,128]{3,2,1,0:T(8,128)S(1)} all-to-all(f32[32,2,8,128]{3,2,1,0:T(8,128)S(1)} %bitcast.8), channel_id=1, replica_groups={{31,30,29,28,27,26,25,24,23,22,21,20,19,18,17,16,15,14,13,12,11,10,9,8,..., dimensions={0} | all-to-all | bytes 524288 | tf_op jit(solution)/shard_map/all_to_all | solution.py:227
  43.5 0.8 %copy.13 = f32[8,8,8,128]{3,1,2,0:T(8,128)} copy(f32[8,8,8,128]{3,2,1,0:T(8,128)S(1)} %bitcast.11) | data formatting | bytes 524288
  (4 shorter events, 0.0 us)
Async XLA Ops:
  0.0 8.9 %collective-permute-start = (bf16[24,1024]{1,0:T(8,128)(2,1)}, bf16[24,1024]{1,0:T(8,128)(2,1)S(1)}, u32[]{:S(2)}, u32[]{:S(2)}) collective-permute-start(bf16[24,1024]{1,0:T(8,128)(2,1)} %rec.1), channel_id=1, source_target_pairs={{0,480},{32,0},{64,32},{96,64},{128,96},{160,128},{192,160},{224,1... | collective-permute-start | bytes 147464 | tf_op jit(solution)/shard_map/ppermute | solution.py:153
  2.9 0.7 %copy-start = (bf16[8,12,16]{2,0,1:T(8,128)(2,1)S(1)}, bf16[8,12,16]{2,0,1:T(8,128)(2,1)}, u32[]{:S(2)}) copy-start(bf16[8,12,16]{2,0,1:T(8,128)(2,1)} %param.6) | copy-start | bytes 9220
  4.4 4.6 %copy-start.1 = (bf16[24,1024]{1,0:T(8,128)(2,1)S(1)}, bf16[24,1024]{1,0:T(8,128)(2,1)}, u32[]{:S(2)}) copy-start(bf16[24,1024]{1,0:T(8,128)(2,1)} %rec.1) | copy-start | bytes 147460
  4.4 12.4 %all-to-all-start = ((bf16[16,16,128]{2,1,0:T(8,128)(2,1)}), bf16[16,16,128]{2,1,0:T(8,128)(2,1)S(1)}, u32[]{:S(2)}, u32[]{:S(2)}) async-start(bf16[16,16,128]{2,1,0:T(8,128)(2,1)} %shard_map.56), calls=%async_computation | async-start | bytes 131072 | tf_op jit(solution)/shard_map/all_to_all | solution.py:157
  9.0 0.7 %copy-start.2 = (s32[256,12]{0,1:T(8,128)S(1)}, s32[256,12]{0,1:T(8,128)}, u32[]{:S(2)}) copy-start(s32[256,12]{0,1:T(8,128)} %param.7) | copy-start | bytes 36868
  9.0 0.7 %copy-start.3 = (s32[256,12]{0,1:T(8,128)S(1)}, s32[256,12]{0,1:T(8,128)}, u32[]{:S(2)}) copy-start(s32[256,12]{0,1:T(8,128)} %param.8) | copy-start | bytes 36868
  9.0 0.7 %copy-start.4 = (s32[256,1]{0,1:T(1,128)S(1)}, s32[256,1]{0,1:T(1,128)}, u32[]{:S(2)}) copy-start(s32[256,1]{0,1:T(1,128)} %param.9) | copy-start | bytes 3076
  9.9 8.9 %collective-permute-start.1 = (bf16[16,1536]{1,0:T(8,128)(2,1)S(1)}, bf16[16,1536]{1,0:T(8,128)(2,1)S(1)}, u32[]{:S(2)}, u32[]{:S(2)}) collective-permute-start(bf16[16,1536]{1,0:T(8,128)(2,1)S(1)} %pad_maximum_fusion), channel_id=1, source_target_pairs={{0,31},{1,0},{2,1},{3,2},{4,3},{5,4},{6,5},{7,6},{8,7},{9,8},{10,9... | collective-permute-start | bytes 147464 | tf_op jit(solution)/shard_map/ppermute | solution.py:153

commit v6 on v5

--- a/solution.py
+++ b/solution.py
@@ -16,6 +16,7 @@
 SCAP = 2
 PAIRS = TPL * SLOTS
 FROM = 16
+RING = [(15 + i) % 16 for i in range(16)]
 F32 = jnp.float32
 BF16 = jnp.bfloat16
 
@@ -113,7 +114,7 @@
     copy = pltpu.make_async_copy(table_v, table, sem)
     copy.start()
     order = [h + i for h in (0, LANES) for i in reversed(range(0, LANES, ROWS))]
-    wave_t = jnp.concatenate([waves[pl.ds(i, ROWS), :].astype(F32) for i in order], axis=0).T
+    wave_t = jnp.concatenate([waves[pl.ds(RING.index(i // ROWS) * ROWS, ROWS), :].astype(F32) for i in order], axis=0).T
     wr[0] = wave_t[:, :LANES]
     wr[1] = wave_t[:, LANES:]
     we[...] = jnp.broadcast_to(jnp.sum(wave_t * wave_t, axis=1, keepdims=True), we.shape)
@@ -154,7 +155,7 @@
 
 
 def gathered(chunks):
-    return lax.all_to_all(chunks, "tm", 0, 0).reshape(L, LANES)
+    return lax.all_to_all(chunks, "tm", 0, 0, axis_index_groups=[RING]).reshape(L, LANES)
 
 
 def local(records, template_waves, channel_lists, moveouts, owner_map):
@@ -173,10 +174,7 @@
     )(jnp.transpose(template_waves, (1, 0, 2)))
     right = shifted(records, "tm", n_tm)
     edge = jnp.concatenate([records[:SPILL], right[:SPILL, :HALO]], axis=1)
-    lists, shifts, owners, edge = lax.optimization_barrier((channel_lists, moveouts, owner_map, edge))
     below = shifted(edge, "chan", n_chan)
-    table = jnp.concatenate([lists, shifts, owners], axis=1)
-    table = lax.dynamic_slice_in_dim(table, lax.axis_index("chan") * TPL, TPL, 0)
     waves = gathered(chunks)
     scalars = [pltpu.SMEM((TPL, 2 * SLOTS + 1), jnp.int32), pltpu.SemaphoreType.DMA]
 
@@ -195,6 +193,9 @@
         compiler_params=params,
         cost_estimate=pl.CostEstimate(flops=200_000_000, bytes_accessed=1_000_000, transcendentals=0),
     )(records, right)
+    lists, shifts, owners, energy = lax.optimization_barrier((channel_lists, moveouts, owner_map, energy))
+    table = jnp.concatenate([lists, shifts, owners], axis=1)
+    table = lax.dynamic_slice_in_dim(table, lax.axis_index("chan") * TPL, TPL, 0)
     part, rows_w, energy_w = pl.pallas_call(
         lambda *refs: own_kernel(ch_dev * n_chan, *refs),
         out_shape=(

time: 44.6 us -> 43.3 us (0.971)
  the two profiles are of different devices: /device:TPU:6 before, /device:TPU:8 now
where the time goes in v6:
time: 43.3 us; the launch traced here: 42.9 us
  starting transfers between devices  20.7 us (48%)
  blocking collectives  15.1 us (35%)
  Pallas kernels  4.67 us (11%)
  local copies, waits for them, and re-layouts  2.26 us (5%)
    all_to_all x1, blocking collectives, local(): lax.all_to_all(outgoing.reshape(n_chan, SCAP, TPL, LANES), 'chan', 0, 0,...  15.1 us
    ppermute x2, starting transfers between devices, shifted(): lax.ppermute(value, axis, [(s, (s - 1) % count) for s in range(count)])  10.9 us
    all_to_all x1, starting transfers between devices, gathered(): lax.all_to_all(chunks, 'tm', 0, 0, axis_index_groups=[RING])  9.75 us
    unnamed x12, local copies, waits for them, and re-layouts  2.24 us
    pallas_call x1, Pallas kernels, local(): pl.pallas_call(lambda *refs: own_kernel(ch_dev * n_chan, *refs), out_shap...  1.98 us
    pallas_call x1, Pallas kernels, local(): pl.pallas_call(lambda *refs: rest_kernel(ch_dev * n_chan, *refs), out_sha...  1.64 us
  transfers between devices with their start and end apart: 3, of which 0 were waited for; matrix products, arithmetic and copies ran while one was open for 0% of the time, Pallas kernels for 7%

profile of v6, /device:TPU:8, one launch (start us, length us, event | category | flops | bytes accessed | tf_op | source)
XLA Modules:
  0.0 42.9 jit_solution(10750388241230557172)
XLA Ops:
  0.0 0.0 collective-permute-start
  0.0 0.0 copy-start
  0.0 0.7 %copy-done = bf16[8,12,16]{2,0,1:T(8,128)(2,1)S(1)} copy-done((bf16[8,12,16]{2,0,1:T(8,128)(2,1)S(1)}, bf16[8,12,16]{2,0,1:T(8,128)(2,1)}, u32[]{:S(2)}) %copy-start) | copy-done | bytes 3096
  0.7 0.7 %shard_map.56 = bf16[16,16,128]{2,1,0:T(8,128)(2,1)} custom-call(bf16[12,8,16]{2,1,0:T(8,128)(2,1)S(1)} %bitcast.10), custom_call_target="tpu_custom_call" | custom-call | tf_op jit(solution)/shard_map/pallas_call | solution.py:168
  1.5 0.0 copy-start.1
  1.5 9.7 %all-to-all-start = ((bf16[16,16,128]{2,1,0:T(8,128)(2,1)}), bf16[16,16,128]{2,1,0:T(8,128)(2,1)S(1)}, u32[]{:S(2)}, u32[]{:S(2)}) async-start(bf16[16,16,128]{2,1,0:T(8,128)(2,1)} %shard_map.56), calls=%async_computation | async-start | bytes 131072 | tf_op jit(solution)/shard_map/all_to_all | solution.py:158
  11.2 0.0 copy-done.1
  11.2 0.0 collective-permute-done.right
  11.3 0.0 copy-start.2
  11.3 0.0 copy-start.3
  11.3 10.9 %collective-permute-start.1 = (bf16[16,1536]{1,0:T(8,128)(2,1)S(1)}, bf16[16,1536]{1,0:T(8,128)(2,1)S(1)}, u32[]{:S(2)}, u32[]{:S(2)}) collective-permute-start(bf16[16,1536]{1,0:T(8,128)(2,1)S(1)} %pad_maximum_fusion), channel_id=1, source_target_pairs={{0,31},{1,0},{2,1},{3,2},{4,3},{5,4},{6,5},{7,6},{8,7},{9,8},{10,9... | collective-permute-start | bytes 147464 | tf_op jit(solution)/shard_map/ppermute | solution.py:154
  22.2 0.3 shard_map.55
  22.6 0.0 copy-start.4
  22.6 0.0 copy-done.2
  22.6 0.0 copy-done.3
  22.6 0.7 %copy-done.4 = s32[256,1]{0,1:T(1,128)S(1)} copy-done((s32[256,1]{0,1:T(1,128)S(1)}, s32[256,1]{0,1:T(1,128)}, u32[]{:S(2)}) %copy-start.4) | copy-done | bytes 1048
  23.2 0.1 fusion.1
  23.3 0.1 copy.10.refs_0_
  23.4 0.0 all-to-all-done
  23.4 2.0 %shard_map.57 = (f32[8,8,128]{2,1,0:T(8,128)S(1)}, f32[2,128,128]{2,1,0:T(8,128)S(1)}, f32[128,128]{1,0:T(8,128)S(1)}) custom-call(s32[8,25]{1,0:T(8,128)S(1)} %copy.10.refs_0_, bf16[384,256]{1,0:T(8,128)(2,1)S(1)} %get-tuple-element.18.refs_1_, f32[384,128]{1,0:T(8,128)S(1)} %get-tuple-element.19.refs_2_, bf16[256,128]{1,0:T(8,128)(2,1)S(1)} %bitcast.9), custom_call_target="tpu_custom_call" | custom-call | flops 1000000000 | bytes 1000000 | tf_op jit(solution)/shard_map/pallas_call | solution.py:199
  25.4 0.0 collective-permute-done.1.refs_3_
  25.4 1.6 %shard_map.58 = f32[64,8,128]{2,1,0:T(8,128)S(1)} custom-call(s32[8,25]{1,0:T(8,128)S(1)} %copy.10.refs_0_, bf16[384,256]{1,0:T(8,128)(2,1)S(1)} %get-tuple-element.18.refs_1_, f32[384,128]{1,0:T(8,128)S(1)} %get-tuple-element.19.refs_2_, bf16[16,1536]{1,0:T(8,128)(2,1)S(1)} %collective-permute-done.1.refs_3_, f32[8,8,128]{2,1,0:T(8,128)S(1)} %get-tuple-element.20.refs_4_, ...), custom_call_target="tpu_custom_call" | custom-call | tf_op jit(solution)/shard_map/pallas_call | solution.py:213
  27.0 15.1 %all_to_all.10 = f32[32,2,8,128]{3,2,1,0:T(8,128)S(1)} all-to-all(f32[32,2,8,128]{3,2,1,0:T(8,128)S(1)} %bitcast.8), channel_id=1, replica_groups={{31,30,29,28,27,26,25,24,23,22,21,20,19,18,17,16,15,14,13,12,11,10,9,8,..., dimensions={0} | all-to-all | bytes 524288 | tf_op jit(solution)/shard_map/all_to_all | solution.py:228
  42.2 0.8 %copy.13 = f32[8,8,8,128]{3,1,2,0:T(8,128)} copy(f32[8,8,8,128]{3,2,1,0:T(8,128)S(1)} %bitcast.11) | data formatting | bytes 524288
  (4 shorter events, 0.0 us)
Async XLA Ops:
  0.0 11.2 %collective-permute-start = (bf16[24,1024]{1,0:T(8,128)(2,1)}, bf16[24,1024]{1,0:T(8,128)(2,1)S(1)}, u32[]{:S(2)}, u32[]{:S(2)}) collective-permute-start(bf16[24,1024]{1,0:T(8,128)(2,1)} %rec.1), channel_id=1, source_target_pairs={{0,480},{32,0},{64,32},{96,64},{128,96},{160,128},{192,160},{224,1... | collective-permute-start | bytes 147464 | tf_op jit(solution)/shard_map/ppermute | solution.py:154
  0.0 0.7 %copy-start = (bf16[8,12,16]{2,0,1:T(8,128)(2,1)S(1)}, bf16[8,12,16]{2,0,1:T(8,128)(2,1)}, u32[]{:S(2)}) copy-start(bf16[8,12,16]{2,0,1:T(8,128)(2,1)} %param.6) | copy-start | bytes 9220
  1.5 9.8 %copy-start.1 = (bf16[24,1024]{1,0:T(8,128)(2,1)S(1)}, bf16[24,1024]{1,0:T(8,128)(2,1)}, u32[]{:S(2)}) copy-start(bf16[24,1024]{1,0:T(8,128)(2,1)} %rec.1) | copy-start | bytes 147460
  1.5 21.9 %all-to-all-start = ((bf16[16,16,128]{2,1,0:T(8,128)(2,1)}), bf16[16,16,128]{2,1,0:T(8,128)(2,1)S(1)}, u32[]{:S(2)}, u32[]{:S(2)}) async-start(bf16[16,16,128]{2,1,0:T(8,128)(2,1)} %shard_map.56), calls=%async_computation | async-start | bytes 131072 | tf_op jit(solution)/shard_map/all_to_all | solution.py:158
  11.3 11.3 %copy-start.2 = (s32[256,12]{0,1:T(8,128)S(1)}, s32[256,12]{0,1:T(8,128)}, u32[]{:S(2)}) copy-start(s32[256,12]{0,1:T(8,128)} %param.7) | copy-start | bytes 36868
  11.3 11.3 %copy-start.3 = (s32[256,12]{0,1:T(8,128)S(1)}, s32[256,12]{0,1:T(8,128)}, u32[]{:S(2)}) copy-start(s32[256,12]{0,1:T(8,128)} %param.8) | copy-start | bytes 36868
  11.3 14.1 %collective-permute-start.1 = (bf16[16,1536]{1,0:T(8,128)(2,1)S(1)}, bf16[16,1536]{1,0:T(8,128)(2,1)S(1)}, u32[]{:S(2)}, u32[]{:S(2)}) collective-permute-start(bf16[16,1536]{1,0:T(8,128)(2,1)S(1)} %pad_maximum_fusion), channel_id=1, source_target_pairs={{0,31},{1,0},{2,1},{3,2},{4,3},{5,4},{6,5},{7,6},{8,7},{9,8},{10,9... | collective-permute-start | bytes 147464 | tf_op jit(solution)/shard_map/ppermute | solution.py:154
  22.6 0.7 %copy-start.4 = (s32[256,1]{0,1:T(1,128)S(1)}, s32[256,1]{0,1:T(1,128)}, u32[]{:S(2)}) copy-start(s32[256,1]{0,1:T(1,128)} %param.9) | copy-start | bytes 3076

commit v7 on v6

--- a/solution.py
+++ b/solution.py
@@ -16,7 +16,7 @@
 SCAP = 2
 PAIRS = TPL * SLOTS
 FROM = 16
-RING = [(15 + i) % 16 for i in range(16)]
+RING = [(15 - i) % 16 for i in range(16)]
 F32 = jnp.float32
 BF16 = jnp.bfloat16
 
@@ -55,7 +55,7 @@
     return pair.astype(BF16), both[:, :LANES] + pr[pl.ds(1, rows), :]
 
 
-def frame_kernel(rec, right, xx, ee, xs, pr):
+def frame_kernel(rec, right, owners, xx, ee, held, xs, pr):
     for b in range(12):
         part, at = (rec, b) if b < 8 else (right, b - 8)
         xs[pl.ds(b, CH, stride=ROWS), :] = part[:, LANES * at : LANES * (at + 1)].astype(F32)
@@ -63,6 +63,7 @@
         xs[pl.ds(b, CH, stride=ROWS), :] = jnp.zeros((CH, LANES), F32)
     xs[pl.ds(CH * ROWS, 8), :] = jnp.zeros((8, LANES), F32)
     xx[...], ee[...] = frame_pairs(xs, pr, CH * ROWS)
+    held[...] = owners[...]
 
 
 def own_slots(k):
@@ -123,9 +124,11 @@
         part[k] = stacked(table, k, range(own_slots(k)), 0, total_chan, xx, ee, wr, we, sh)
 
 
-def rest_kernel(total_chan, table_v, own_xx, own_ee, below, part, wr, we, out, xs, pr, xx, ee, sh, table, sem):
+def rest_kernel(total_chan, table_v, owners_v, own_xx, own_ee, below, part, wr, we, out, xs, pr, xx, ee, sh, table, sem, owners, owner_sem):
     copy = pltpu.make_async_copy(table_v, table, sem)
     copy.start()
+    owner_copy = pltpu.make_async_copy(owners_v, owners, owner_sem)
+    owner_copy.start()
     for b in range(12):
         xs[pl.ds(b, SPILL, stride=ROWS), :] = below[:, LANES * b : LANES * (b + 1)].astype(F32)
     for b in range(12, ROWS):
@@ -140,13 +143,15 @@
 
     out[...] = jnp.zeros_like(out)
     copy.wait()
+    owner_copy.wait()
+    first = lax.axis_index("chan") * TPL
     for k in range(TPL):
         slots = range(own_slots(k), SLOTS)
         total = part[k] + stacked(table, k, slots, FROM, total_chan, xx, ee, wr, we, sh)
-        owner = table[k, 2 * SLOTS]
+        owner = owners[0, first + k]
         rank = jnp.int32(0)
         for q in range(k):
-            rank = rank + jnp.where(table[q, 2 * SLOTS] == owner, 1, 0)
+            rank = rank + jnp.where(owners[0, first + q] == owner, 1, 0)
         out[(out.shape[0] // SCAP - 1 - owner) * SCAP + rank] = total
 
 
@@ -176,25 +181,26 @@
     edge = jnp.concatenate([records[:SPILL], right[:SPILL, :HALO]], axis=1)
     below = shifted(edge, "chan", n_chan)
     waves = gathered(chunks)
-    scalars = [pltpu.SMEM((TPL, 2 * SLOTS + 1), jnp.int32), pltpu.SemaphoreType.DMA]
+    scalars = [pltpu.SMEM((TPL, 2 * SLOTS), jnp.int32), pltpu.SemaphoreType.DMA]
 
     def scratch(*shape):
         return pltpu.VMEM(shape, F32)
 
-    frames, energy = pl.pallas_call(
+    frames, energy, owners = pl.pallas_call(
         frame_kernel,
         out_shape=(
             jax.ShapeDtypeStruct((CH * ROWS, 2 * LANES), BF16),
             jax.ShapeDtypeStruct((CH * ROWS, LANES), F32),
+            jax.ShapeDtypeStruct((1, owner_map.shape[0]), jnp.int32),
         ),
-        in_specs=[vmem] * 2,
-        out_specs=(vmem, vmem),
+        in_specs=[vmem] * 3,
+        out_specs=(vmem,) * 3,
         scratch_shapes=[scratch(CH * ROWS + 8, LANES)] * 2,
         compiler_params=params,
         cost_estimate=pl.CostEstimate(flops=200_000_000, bytes_accessed=1_000_000, transcendentals=0),
-    )(records, right)
-    lists, shifts, owners, energy = lax.optimization_barrier((channel_lists, moveouts, owner_map, energy))
-    table = jnp.concatenate([lists, shifts, owners], axis=1)
+    )(records, right, owner_map.T)
+    lists, shifts, energy = lax.optimization_barrier((channel_lists, moveouts, energy))
+    table = jnp.concatenate([lists, shifts], axis=1)
     table = lax.dynamic_slice_in_dim(table, lax.axis_index("chan") * TPL, TPL, 0)
     part, rows_w, energy_w = pl.pallas_call(
         lambda *refs: own_kernel(ch_dev * n_chan, *refs),
@@ -213,7 +219,7 @@
     outgoing = pl.pallas_call(
         lambda *refs: rest_kernel(ch_dev * n_chan, *refs),
         out_shape=jax.ShapeDtypeStruct((n_chan * SCAP, TPL, LANES), F32),
-        in_specs=[vmem] * 7,
+        in_specs=[vmem] * 8,
         out_specs=vmem,
         scratch_shapes=[
             scratch(SPILL * ROWS + 8, LANES),
@@ -222,9 +228,10 @@
             scratch(late_rows, LANES),
             scratch(SLOTS, ROWS, LANES),
         ]
-        + scalars,
-        compiler_params=params,
-    )(table, frames, energy, below, part, rows_w, energy_w)
+        + scalars
+        + [pltpu.SMEM((1, owner_map.shape[0]), jnp.int32), pltpu.SemaphoreType.DMA],
+        compiler_params=params,
+    )(table, owners, frames, energy, below, part, rows_w, energy_w)
     incoming = lax.all_to_all(
         outgoing.reshape(n_chan, SCAP, TPL, LANES),
         "chan",

time: 43.3 us -> 43.2 us (level)
  no operation moved by 1% of the time
where the time goes in v7:
time: 43.2 us; the launch traced here: 42.8 us
  starting transfers between devices  20.7 us (48%)
  blocking collectives  15.2 us (35%)
  Pallas kernels  4.69 us (11%)
  local copies, waits for them, and re-layouts  1.97 us (5%)
    all_to_all x1, blocking collectives, local(): lax.all_to_all(outgoing.reshape(n_chan, SCAP, TPL, LANES), 'chan', 0, 0,...  15.2 us
    ppermute x2, starting transfers between devices, shifted(): lax.ppermute(value, axis, [(s, (s - 1) % count) for s in range(count)])  10.9 us
    all_to_all x1, starting transfers between devices, gathered(): lax.all_to_all(chunks, 'tm', 0, 0, axis_index_groups=[RING])  9.79 us
    pallas_call x1, Pallas kernels, local(): pl.pallas_call(lambda *refs: own_kernel(ch_dev * n_chan, *refs), out_shap...  1.98 us
    unnamed x12, local copies, waits for them, and re-layouts  1.95 us
    pallas_call x1, Pallas kernels, local(): pl.pallas_call(lambda *refs: rest_kernel(ch_dev * n_chan, *refs), out_sha...  1.67 us
  transfers between devices with their start and end apart: 3, of which 0 were waited for; matrix products, arithmetic and copies ran while one was open for 0% of the time, Pallas kernels for 7%

profile of v7, /device:TPU:8, one launch (start us, length us, event | category | flops | bytes accessed | tf_op | source)
XLA Modules:
  0.0 42.8 jit_solution(7153365555955092687)
XLA Ops:
  0.0 0.0 collective-permute-start
  0.0 0.0 copy-start
  0.0 0.7 %copy-done = bf16[8,12,16]{2,0,1:T(8,128)(2,1)S(1)} copy-done((bf16[8,12,16]{2,0,1:T(8,128)(2,1)S(1)}, bf16[8,12,16]{2,0,1:T(8,128)(2,1)}, u32[]{:S(2)}) %copy-start) | copy-done | bytes 3096
  0.7 0.7 %shard_map.56 = bf16[16,16,128]{2,1,0:T(8,128)(2,1)} custom-call(bf16[12,8,16]{2,1,0:T(8,128)(2,1)S(1)} %bitcast.11), custom_call_target="tpu_custom_call" | custom-call | tf_op jit(solution)/shard_map/pallas_call | solution.py:173
  1.5 0.0 copy-start.1
  1.5 9.8 %all-to-all-start = ((bf16[16,16,128]{2,1,0:T(8,128)(2,1)}), bf16[16,16,128]{2,1,0:T(8,128)(2,1)S(1)}, u32[]{:S(2)}, u32[]{:S(2)}) async-start(bf16[16,16,128]{2,1,0:T(8,128)(2,1)} %shard_map.56), calls=%async_computation | async-start | bytes 131072 | tf_op jit(solution)/shard_map/all_to_all | solution.py:163
  11.2 0.0 copy-done.1
  11.3 0.0 collective-permute-done.right
  11.3 0.0 copy-start.2
  11.3 10.9 %collective-permute-start.1 = (bf16[16,1536]{1,0:T(8,128)(2,1)S(1)}, bf16[16,1536]{1,0:T(8,128)(2,1)S(1)}, u32[]{:S(2)}, u32[]{:S(2)}) collective-permute-start(bf16[16,1536]{1,0:T(8,128)(2,1)S(1)} %pad_maximum_fusion), channel_id=1, source_target_pairs={{0,31},{1,0},{2,1},{3,2},{4,3},{5,4},{6,5},{7,6},{8,7},{9,8},{10,9... | collective-permute-start | bytes 147464 | tf_op jit(solution)/shard_map/ppermute | solution.py:159
  22.2 0.0 copy-done.2
  22.3 0.0 copy-start.3
  22.3 0.0 copy-start.4
  22.3 0.3 shard_map.55
  22.6 0.4 copy-done.3
  23.0 0.0 copy-done.4
  23.0 0.1 fusion
  23.1 0.1 copy.9.refs_0_
  23.1 0.0 all-to-all-done
  23.1 2.0 %shard_map.57 = (f32[8,8,128]{2,1,0:T(8,128)S(1)}, f32[2,128,128]{2,1,0:T(8,128)S(1)}, f32[128,128]{1,0:T(8,128)S(1)}) custom-call(s32[8,24]{1,0:T(8,128)S(1)} %copy.9.refs_0_, bf16[384,256]{1,0:T(8,128)(2,1)S(1)} %get-tuple-element.18.refs_1_.refs_2_, f32[384,128]{1,0:T(8,128)S(1)} %get-tuple-element.19.refs_2_.refs_3_, bf16[256,128]{1,0:T(8,128)(2,1)S(1)} %bitcast.10), custom_call_target="tpu_custom_call" | custom-call | flops 1000000000 | bytes 1000000 | tf_op jit(solution)/shard_map/pallas_call | solution.py:205
  25.1 0.0 collective-permute-done.1.refs_4_
  25.1 1.7 %shard_map.58 = f32[64,8,128]{2,1,0:T(8,128)S(1)} custom-call(s32[8,24]{1,0:T(8,128)S(1)} %copy.9.refs_0_, s32[1,256]{1,0:T(1,128)S(1)} %get-tuple-element.17.refs_1_, bf16[384,256]{1,0:T(8,128)(2,1)S(1)} %get-tuple-element.18.refs_1_.refs_2_, f32[384,128]{1,0:T(8,128)S(1)} %get-tuple-element.19.refs_2_.refs_3_, ...), custom_call_target="tpu_custom_call" | custom-call | tf_op jit(solution)/shard_map/pallas_call | solution.py:219
  26.8 15.2 %all_to_all.10 = f32[32,2,8,128]{3,2,1,0:T(8,128)S(1)} all-to-all(f32[32,2,8,128]{3,2,1,0:T(8,128)S(1)} %bitcast.9), channel_id=1, replica_groups={{31,30,29,28,27,26,25,24,23,22,21,20,19,18,17,16,15,14,13,12,11,10,9,8,..., dimensions={0} | all-to-all | bytes 524288 | tf_op jit(solution)/shard_map/all_to_all | solution.py:235
  42.0 0.8 %copy.12 = f32[8,8,8,128]{3,1,2,0:T(8,128)} copy(f32[8,8,8,128]{3,2,1,0:T(8,128)S(1)} %bitcast.13) | data formatting | bytes 524288
  (4 shorter events, 0.0 us)
Async XLA Ops:
  0.0 11.3 %collective-permute-start = (bf16[24,1024]{1,0:T(8,128)(2,1)}, bf16[24,1024]{1,0:T(8,128)(2,1)S(1)}, u32[]{:S(2)}, u32[]{:S(2)}) collective-permute-start(bf16[24,1024]{1,0:T(8,128)(2,1)} %rec.1), channel_id=1, source_target_pairs={{0,480},{32,0},{64,32},{96,64},{128,96},{160,128},{192,160},{224,1... | collective-permute-start | bytes 147464 | tf_op jit(solution)/shard_map/ppermute | solution.py:159
  0.0 0.7 %copy-start = (bf16[8,12,16]{2,0,1:T(8,128)(2,1)S(1)}, bf16[8,12,16]{2,0,1:T(8,128)(2,1)}, u32[]{:S(2)}) copy-start(bf16[8,12,16]{2,0,1:T(8,128)(2,1)} %param.6) | copy-start | bytes 9220
  1.5 9.8 %copy-start.1 = (bf16[24,1024]{1,0:T(8,128)(2,1)S(1)}, bf16[24,1024]{1,0:T(8,128)(2,1)}, u32[]{:S(2)}) copy-start(bf16[24,1024]{1,0:T(8,128)(2,1)} %rec.1) | copy-start | bytes 147460
  1.5 21.7 %all-to-all-start = ((bf16[16,16,128]{2,1,0:T(8,128)(2,1)}), bf16[16,16,128]{2,1,0:T(8,128)(2,1)S(1)}, u32[]{:S(2)}, u32[]{:S(2)}) async-start(bf16[16,16,128]{2,1,0:T(8,128)(2,1)} %shard_map.56), calls=%async_computation | async-start | bytes 131072 | tf_op jit(solution)/shard_map/all_to_all | solution.py:163
  11.3 10.9 %copy-start.2 = (s32[256,1]{0,1:T(1,128)S(1)}, s32[256,1]{0,1:T(1,128)}, u32[]{:S(2)}) copy-start(s32[256,1]{0,1:T(1,128)} %param.9) | copy-start | bytes 3076
  11.3 13.8 %collective-permute-start.1 = (bf16[16,1536]{1,0:T(8,128)(2,1)S(1)}, bf16[16,1536]{1,0:T(8,128)(2,1)S(1)}, u32[]{:S(2)}, u32[]{:S(2)}) collective-permute-start(bf16[16,1536]{1,0:T(8,128)(2,1)S(1)} %pad_maximum_fusion), channel_id=1, source_target_pairs={{0,31},{1,0},{2,1},{3,2},{4,3},{5,4},{6,5},{7,6},{8,7},{9,8},{10,9... | collective-permute-start | bytes 147464 | tf_op jit(solution)/shard_map/ppermute | solution.py:159
  22.3 0.7 %copy-start.3 = (s32[256,12]{0,1:T(8,128)S(1)}, s32[256,12]{0,1:T(8,128)}, u32[]{:S(2)}) copy-start(s32[256,12]{0,1:T(8,128)} %param.7) | copy-start | bytes 36868
  22.3 0.7 %copy-start.4 = (s32[256,12]{0,1:T(8,128)S(1)}, s32[256,12]{0,1:T(8,128)}, u32[]{:S(2)}) copy-start(s32[256,12]{0,1:T(8,128)} %param.8) | copy-start | bytes 36868

commit v8 on v7

--- a/solution.py
+++ b/solution.py
@@ -55,7 +55,7 @@
     return pair.astype(BF16), both[:, :LANES] + pr[pl.ds(1, rows), :]
 
 
-def frame_kernel(rec, right, owners, xx, ee, held, xs, pr):
+def frame_kernel(rec, right, owners, lists, shifts, xx, ee, held, both, xs, pr):
     for b in range(12):
         part, at = (rec, b) if b < 8 else (right, b - 8)
         xs[pl.ds(b, CH, stride=ROWS), :] = part[:, LANES * at : LANES * (at + 1)].astype(F32)
@@ -64,6 +64,10 @@
     xs[pl.ds(CH * ROWS, 8), :] = jnp.zeros((8, LANES), F32)
     xx[...], ee[...] = frame_pairs(xs, pr, CH * ROWS)
     held[...] = owners[...]
+    both[pl.ds(0, SLOTS), :] = lists[...]
+    both[pl.ds(ROWS, SLOTS), :] = shifts[...]
+    both[pl.ds(SLOTS, ROWS - SLOTS), :] = jnp.zeros((ROWS - SLOTS, both.shape[1]), jnp.int32)
+    both[pl.ds(ROWS + SLOTS, ROWS - SLOTS), :] = jnp.zeros((ROWS - SLOTS, both.shape[1]), jnp.int32)
 
 
 def own_slots(k):
@@ -89,7 +93,7 @@
         place = jnp.where(place < 0, place + total_chan, place) - first_row
         place = jnp.where(valid, place, 0)
         start = pl.multiple_of(place * ROWS, ROWS)
-        shift = table[k, SLOTS + j]
+        shift = table[k, ROWS + j]
         lanes, rows = shift & (LANES - 1), shift >> 7
         first, second = circulant(p, 0), circulant(p, 1)
         band = jnp.concatenate(
@@ -181,27 +185,26 @@
     edge = jnp.concatenate([records[:SPILL], right[:SPILL, :HALO]], axis=1)
     below = shifted(edge, "chan", n_chan)
     waves = gathered(chunks)
-    scalars = [pltpu.SMEM((TPL, 2 * SLOTS), jnp.int32), pltpu.SemaphoreType.DMA]
+    scalars = [pltpu.SMEM((TPL, 2 * ROWS), jnp.int32), pltpu.SemaphoreType.DMA]
 
     def scratch(*shape):
         return pltpu.VMEM(shape, F32)
 
-    frames, energy, owners = pl.pallas_call(
+    frames, energy, owners, both = pl.pallas_call(
         frame_kernel,
         out_shape=(
             jax.ShapeDtypeStruct((CH * ROWS, 2 * LANES), BF16),
             jax.ShapeDtypeStruct((CH * ROWS, LANES), F32),
             jax.ShapeDtypeStruct((1, owner_map.shape[0]), jnp.int32),
+            jax.ShapeDtypeStruct((2 * ROWS, owner_map.shape[0]), jnp.int32),
         ),
-        in_specs=[vmem] * 3,
-        out_specs=(vmem,) * 3,
+        in_specs=[vmem] * 5,
+        out_specs=(vmem,) * 4,
         scratch_shapes=[scratch(CH * ROWS + 8, LANES)] * 2,
         compiler_params=params,
         cost_estimate=pl.CostEstimate(flops=200_000_000, bytes_accessed=1_000_000, transcendentals=0),
-    )(records, right, owner_map.T)
-    lists, shifts, energy = lax.optimization_barrier((channel_lists, moveouts, energy))
-    table = jnp.concatenate([lists, shifts], axis=1)
-    table = lax.dynamic_slice_in_dim(table, lax.axis_index("chan") * TPL, TPL, 0)
+    )(records, right, owner_map.T, channel_lists.T, moveouts.T)
+    table = lax.dynamic_slice_in_dim(both, lax.axis_index("chan") * TPL, TPL, 1).T
     part, rows_w, energy_w = pl.pallas_call(
         lambda *refs: own_kernel(ch_dev * n_chan, *refs),
         out_shape=(

time: 43.2 us -> 43.3 us (level)
    unnamed x12 -> x11, local copies, waits for them, and re-layouts: 1.95 us -> 2.16 us
where the time goes in v8:
time: 43.3 us; the launch traced here: 42.9 us
  starting transfers between devices  20.7 us (48%)
  blocking collectives  15.1 us (35%)
  Pallas kernels  4.69 us (11%)
  local copies, waits for them, and re-layouts  2.29 us (5%)
    all_to_all x1, blocking collectives, local(): lax.all_to_all(outgoing.reshape(n_chan, SCAP, TPL, LANES), 'chan', 0, 0,...  15.1 us
    ppermute x2, starting transfers between devices, shifted(): lax.ppermute(value, axis, [(s, (s - 1) % count) for s in range(count)])  10.9 us
    all_to_all x1, starting transfers between devices, gathered(): lax.all_to_all(chunks, 'tm', 0, 0, axis_index_groups=[RING])  9.79 us
    unnamed x11, local copies, waits for them, and re-layouts  2.16 us
    pallas_call x1, Pallas kernels, local(): pl.pallas_call(lambda *refs: own_kernel(ch_dev * n_chan, *refs), out_shap...  1.98 us
    pallas_call x1, Pallas kernels, local(): pl.pallas_call(lambda *refs: rest_kernel(ch_dev * n_chan, *refs), out_sha...  1.67 us
  transfers between devices with their start and end apart: 3, of which 0 were waited for; matrix products, arithmetic and copies ran while one was open for 0% of the time, Pallas kernels for 7%

profile of v8, /device:TPU:8, one launch (start us, length us, event | category | flops | bytes accessed | tf_op | source)
XLA Modules:
  0.0 42.9 jit_solution(13577097107504878946)
XLA Ops:
  0.0 0.0 collective-permute-start
  0.0 0.0 copy-start
  0.0 0.7 %copy-done = bf16[8,12,16]{2,0,1:T(8,128)(2,1)S(1)} copy-done((bf16[8,12,16]{2,0,1:T(8,128)(2,1)S(1)}, bf16[8,12,16]{2,0,1:T(8,128)(2,1)}, u32[]{:S(2)}) %copy-start) | copy-done | bytes 3096
  0.7 0.7 %shard_map.56 = bf16[16,16,128]{2,1,0:T(8,128)(2,1)} custom-call(bf16[12,8,16]{2,1,0:T(8,128)(2,1)S(1)} %bitcast.15), custom_call_target="tpu_custom_call" | custom-call | tf_op jit(solution)/shard_map/pallas_call | solution.py:177
  1.5 0.0 copy-start.1
  1.5 9.8 %all-to-all-start = ((bf16[16,16,128]{2,1,0:T(8,128)(2,1)}), bf16[16,16,128]{2,1,0:T(8,128)(2,1)S(1)}, u32[]{:S(2)}, u32[]{:S(2)}) async-start(bf16[16,16,128]{2,1,0:T(8,128)(2,1)} %shard_map.56), calls=%async_computation | async-start | bytes 131072 | tf_op jit(solution)/shard_map/all_to_all | solution.py:167
  11.2 0.0 copy-done.1
  11.3 0.0 collective-permute-done.right
  11.3 0.0 copy-start.2
  11.3 0.0 copy-start.3
  11.3 10.9 %collective-permute-start.1 = (bf16[16,1536]{1,0:T(8,128)(2,1)S(1)}, bf16[16,1536]{1,0:T(8,128)(2,1)S(1)}, u32[]{:S(2)}, u32[]{:S(2)}) collective-permute-start(bf16[16,1536]{1,0:T(8,128)(2,1)S(1)} %pad_maximum_fusion), channel_id=1, source_target_pairs={{0,31},{1,0},{2,1},{3,2},{4,3},{5,4},{6,5},{7,6},{8,7},{9,8},{10,9... | collective-permute-start | bytes 147464 | tf_op jit(solution)/shard_map/ppermute | solution.py:163
  22.3 0.0 copy-start.4
  22.3 0.0 copy-done.2
  22.3 0.0 copy-done.3
  22.3 0.7 %copy-done.4 = s32[256,1]{0,1:T(1,128)S(1)} copy-done((s32[256,1]{0,1:T(1,128)S(1)}, s32[256,1]{0,1:T(1,128)}, u32[]{:S(2)}) %copy-start.4) | copy-done | bytes 1048
  22.9 0.3 shard_map.55
  23.3 0.1 copy.6
  23.4 0.0 all-to-all-done
  23.4 2.0 %shard_map.57 = (f32[8,8,128]{2,1,0:T(8,128)S(1)}, f32[2,128,128]{2,1,0:T(8,128)S(1)}, f32[128,128]{1,0:T(8,128)S(1)}) custom-call(s32[8,32]{1,0:T(8,128)S(1)} %dynamic-slice_bitcast_fusion.refs_0_, bf16[384,256]{1,0:T(8,128)(2,1)S(1)} %get-tuple-element.14.refs_1_.refs_2_, f32[384,128]{1,0:T(8,128)S(1)} %get-tuple-element.15.refs_2_.refs_3_, ...), custom_call_target="tpu_custom_call" | custom-call | flops 1000000000 | bytes 1000000 | tf_op jit(solution)/shard_map/pallas_call | solution.py:208
  25.4 0.0 collective-permute-done.1.refs_4_
  25.4 1.7 %shard_map.58 = f32[64,8,128]{2,1,0:T(8,128)S(1)} custom-call(s32[8,32]{1,0:T(8,128)S(1)} %dynamic-slice_bitcast_fusion.refs_0_, s32[1,256]{1,0:T(1,128)S(1)} %get-tuple-element.13.refs_1_, bf16[384,256]{1,0:T(8,128)(2,1)S(1)} %get-tuple-element.14.refs_1_.refs_2_, f32[384,128]{1,0:T(8,128)S(1)} %get-tuple-element.15.refs_2_.refs_3_, ...), custom_call_target="tpu_custom_call" | custom-call | tf_op jit(solution)/shard_map/pallas_call | solution.py:222
  27.1 15.1 %all_to_all.10 = f32[32,2,8,128]{3,2,1,0:T(8,128)S(1)} all-to-all(f32[32,2,8,128]{3,2,1,0:T(8,128)S(1)} %bitcast.13), channel_id=1, replica_groups={{31,30,29,28,27,26,25,24,23,22,21,20,19,18,17,16,15,14,13,12,11,10,9,8,..., dimensions={0} | all-to-all | bytes 524288 | tf_op jit(solution)/shard_map/all_to_all | solution.py:238
  42.2 0.8 %copy.9 = f32[8,8,8,128]{3,1,2,0:T(8,128)} copy(f32[8,8,8,128]{3,2,1,0:T(8,128)S(1)} %bitcast.19) | data formatting | bytes 524288
  (5 shorter events, 0.0 us)
Async XLA Ops:
  0.0 11.3 %collective-permute-start = (bf16[24,1024]{1,0:T(8,128)(2,1)}, bf16[24,1024]{1,0:T(8,128)(2,1)S(1)}, u32[]{:S(2)}, u32[]{:S(2)}) collective-permute-start(bf16[24,1024]{1,0:T(8,128)(2,1)} %rec.1), channel_id=1, source_target_pairs={{0,480},{32,0},{64,32},{96,64},{128,96},{160,128},{192,160},{224,1... | collective-permute-start | bytes 147464 | tf_op jit(solution)/shard_map/ppermute | solution.py:163
  0.0 0.7 %copy-start = (bf16[8,12,16]{2,0,1:T(8,128)(2,1)S(1)}, bf16[8,12,16]{2,0,1:T(8,128)(2,1)}, u32[]{:S(2)}) copy-start(bf16[8,12,16]{2,0,1:T(8,128)(2,1)} %param.6) | copy-start | bytes 9220
  1.5 9.8 %copy-start.1 = (bf16[24,1024]{1,0:T(8,128)(2,1)S(1)}, bf16[24,1024]{1,0:T(8,128)(2,1)}, u32[]{:S(2)}) copy-start(bf16[24,1024]{1,0:T(8,128)(2,1)} %rec.1) | copy-start | bytes 147460
  1.5 21.9 %all-to-all-start = ((bf16[16,16,128]{2,1,0:T(8,128)(2,1)}), bf16[16,16,128]{2,1,0:T(8,128)(2,1)S(1)}, u32[]{:S(2)}, u32[]{:S(2)}) async-start(bf16[16,16,128]{2,1,0:T(8,128)(2,1)} %shard_map.56), calls=%async_computation | async-start | bytes 131072 | tf_op jit(solution)/shard_map/all_to_all | solution.py:167
  11.3 11.0 %copy-start.2 = (s32[256,12]{0,1:T(8,128)S(1)}, s32[256,12]{0,1:T(8,128)}, u32[]{:S(2)}) copy-start(s32[256,12]{0,1:T(8,128)} %param.7) | copy-start | bytes 36868
  11.3 11.0 %copy-start.3 = (s32[256,12]{0,1:T(8,128)S(1)}, s32[256,12]{0,1:T(8,128)}, u32[]{:S(2)}) copy-start(s32[256,12]{0,1:T(8,128)} %param.8) | copy-start | bytes 36868
  11.3 14.1 %collective-permute-start.1 = (bf16[16,1536]{1,0:T(8,128)(2,1)S(1)}, bf16[16,1536]{1,0:T(8,128)(2,1)S(1)}, u32[]{:S(2)}, u32[]{:S(2)}) collective-permute-start(bf16[16,1536]{1,0:T(8,128)(2,1)S(1)} %pad_maximum_fusion), channel_id=1, source_target_pairs={{0,31},{1,0},{2,1},{3,2},{4,3},{5,4},{6,5},{7,6},{8,7},{9,8},{10,9... | collective-permute-start | bytes 147464 | tf_op jit(solution)/shard_map/ppermute | solution.py:163
  22.3 0.7 %copy-start.4 = (s32[256,1]{0,1:T(1,128)S(1)}, s32[256,1]{0,1:T(1,128)}, u32[]{:S(2)}) copy-start(s32[256,1]{0,1:T(1,128)} %param.9) | copy-start | bytes 3076

commit v9 on v7

--- a/solution.py
+++ b/solution.py
@@ -15,7 +15,7 @@
 CH = 24
 SCAP = 2
 PAIRS = TPL * SLOTS
-FROM = 16
+FROM = 19
 RING = [(15 - i) % 16 for i in range(16)]
 F32 = jnp.float32
 BF16 = jnp.bfloat16

time: 43.2 us -> 43.2 us (level)
  no operation moved by 1% of the time
where the time goes in v9:
time: 43.2 us; the launch traced here: 42.8 us
  starting transfers between devices  20.7 us (48%)
  blocking collectives  15.2 us (35%)
  Pallas kernels  4.69 us (11%)
  local copies, waits for them, and re-layouts  1.97 us (5%)
    all_to_all x1, blocking collectives, local(): lax.all_to_all(outgoing.reshape(n_chan, SCAP, TPL, LANES), 'chan', 0, 0,...  15.2 us
    ppermute x2, starting transfers between devices, shifted(): lax.ppermute(value, axis, [(s, (s - 1) % count) for s in range(count)])  10.9 us
    all_to_all x1, starting transfers between devices, gathered(): lax.all_to_all(chunks, 'tm', 0, 0, axis_index_groups=[RING])  9.79 us
    pallas_call x1, Pallas kernels, local(): pl.pallas_call(lambda *refs: own_kernel(ch_dev * n_chan, *refs), out_shap...  1.98 us
    unnamed x12, local copies, waits for them, and re-layouts  1.95 us
    pallas_call x1, Pallas kernels, local(): pl.pallas_call(lambda *refs: rest_kernel(ch_dev * n_chan, *refs), out_sha...  1.67 us
  transfers between devices with their start and end apart: 3, of which 0 were waited for; matrix products, arithmetic and copies ran while one was open for 0% of the time, Pallas kernels for 7%

profile of v9, /device:TPU:8, one launch (start us, length us, event | category | flops | bytes accessed | tf_op | source)
XLA Modules:
  0.0 42.8 jit_solution(4408229183139625303)
XLA Ops:
  0.0 0.0 collective-permute-start
  0.0 0.0 copy-start
  0.0 0.7 %copy-done = bf16[8,12,16]{2,0,1:T(8,128)(2,1)S(1)} copy-done((bf16[8,12,16]{2,0,1:T(8,128)(2,1)S(1)}, bf16[8,12,16]{2,0,1:T(8,128)(2,1)}, u32[]{:S(2)}) %copy-start) | copy-done | bytes 3096
  0.7 0.7 %shard_map.56 = bf16[16,16,128]{2,1,0:T(8,128)(2,1)} custom-call(bf16[12,8,16]{2,1,0:T(8,128)(2,1)S(1)} %bitcast.11), custom_call_target="tpu_custom_call" | custom-call | tf_op jit(solution)/shard_map/pallas_call | solution.py:173
  1.5 0.0 copy-start.1
  1.5 9.8 %all-to-all-start = ((bf16[16,16,128]{2,1,0:T(8,128)(2,1)}), bf16[16,16,128]{2,1,0:T(8,128)(2,1)S(1)}, u32[]{:S(2)}, u32[]{:S(2)}) async-start(bf16[16,16,128]{2,1,0:T(8,128)(2,1)} %shard_map.56), calls=%async_computation | async-start | bytes 131072 | tf_op jit(solution)/shard_map/all_to_all | solution.py:163
  11.2 0.0 copy-done.1
  11.3 0.0 collective-permute-done.right
  11.3 0.0 copy-start.2
  11.3 10.9 %collective-permute-start.1 = (bf16[16,1536]{1,0:T(8,128)(2,1)S(1)}, bf16[16,1536]{1,0:T(8,128)(2,1)S(1)}, u32[]{:S(2)}, u32[]{:S(2)}) collective-permute-start(bf16[16,1536]{1,0:T(8,128)(2,1)S(1)} %pad_maximum_fusion), channel_id=1, source_target_pairs={{0,31},{1,0},{2,1},{3,2},{4,3},{5,4},{6,5},{7,6},{8,7},{9,8},{10,9... | collective-permute-start | bytes 147464 | tf_op jit(solution)/shard_map/ppermute | solution.py:159
  22.2 0.0 copy-done.2
  22.3 0.0 copy-start.3
  22.3 0.0 copy-start.4
  22.3 0.3 shard_map.55
  22.6 0.4 copy-done.3
  23.0 0.0 copy-done.4
  23.0 0.1 fusion
  23.1 0.1 copy.9.refs_0_
  23.1 0.0 all-to-all-done
  23.1 2.0 %shard_map.57 = (f32[8,8,128]{2,1,0:T(8,128)S(1)}, f32[2,128,128]{2,1,0:T(8,128)S(1)}, f32[128,128]{1,0:T(8,128)S(1)}) custom-call(s32[8,24]{1,0:T(8,128)S(1)} %copy.9.refs_0_, bf16[384,256]{1,0:T(8,128)(2,1)S(1)} %get-tuple-element.18.refs_1_.refs_2_, f32[384,128]{1,0:T(8,128)S(1)} %get-tuple-element.19.refs_2_.refs_3_, bf16[256,128]{1,0:T(8,128)(2,1)S(1)} %bitcast.10), custom_call_target="tpu_custom_call" | custom-call | flops 1000000000 | bytes 1000000 | tf_op jit(solution)/shard_map/pallas_call | solution.py:205
  25.1 0.0 collective-permute-done.1.refs_4_
  25.1 1.7 %shard_map.58 = f32[64,8,128]{2,1,0:T(8,128)S(1)} custom-call(s32[8,24]{1,0:T(8,128)S(1)} %copy.9.refs_0_, s32[1,256]{1,0:T(1,128)S(1)} %get-tuple-element.17.refs_1_, bf16[384,256]{1,0:T(8,128)(2,1)S(1)} %get-tuple-element.18.refs_1_.refs_2_, f32[384,128]{1,0:T(8,128)S(1)} %get-tuple-element.19.refs_2_.refs_3_, ...), custom_call_target="tpu_custom_call" | custom-call | tf_op jit(solution)/shard_map/pallas_call | solution.py:219
  26.8 15.2 %all_to_all.10 = f32[32,2,8,128]{3,2,1,0:T(8,128)S(1)} all-to-all(f32[32,2,8,128]{3,2,1,0:T(8,128)S(1)} %bitcast.9), channel_id=1, replica_groups={{31,30,29,28,27,26,25,24,23,22,21,20,19,18,17,16,15,14,13,12,11,10,9,8,..., dimensions={0} | all-to-all | bytes 524288 | tf_op jit(solution)/shard_map/all_to_all | solution.py:235
  42.0 0.8 %copy.12 = f32[8,8,8,128]{3,1,2,0:T(8,128)} copy(f32[8,8,8,128]{3,2,1,0:T(8,128)S(1)} %bitcast.13) | data formatting | bytes 524288
  (4 shorter events, 0.0 us)
Async XLA Ops:
  0.0 11.3 %collective-permute-start = (bf16[24,1024]{1,0:T(8,128)(2,1)}, bf16[24,1024]{1,0:T(8,128)(2,1)S(1)}, u32[]{:S(2)}, u32[]{:S(2)}) collective-permute-start(bf16[24,1024]{1,0:T(8,128)(2,1)} %rec.1), channel_id=1, source_target_pairs={{0,480},{32,0},{64,32},{96,64},{128,96},{160,128},{192,160},{224,1... | collective-permute-start | bytes 147464 | tf_op jit(solution)/shard_map/ppermute | solution.py:159
  0.0 0.7 %copy-start = (bf16[8,12,16]{2,0,1:T(8,128)(2,1)S(1)}, bf16[8,12,16]{2,0,1:T(8,128)(2,1)}, u32[]{:S(2)}) copy-start(bf16[8,12,16]{2,0,1:T(8,128)(2,1)} %param.6) | copy-start | bytes 9220
  1.5 9.8 %copy-start.1 = (bf16[24,1024]{1,0:T(8,128)(2,1)S(1)}, bf16[24,1024]{1,0:T(8,128)(2,1)}, u32[]{:S(2)}) copy-start(bf16[24,1024]{1,0:T(8,128)(2,1)} %rec.1) | copy-start | bytes 147460
  1.5 21.7 %all-to-all-start = ((bf16[16,16,128]{2,1,0:T(8,128)(2,1)}), bf16[16,16,128]{2,1,0:T(8,128)(2,1)S(1)}, u32[]{:S(2)}, u32[]{:S(2)}) async-start(bf16[16,16,128]{2,1,0:T(8,128)(2,1)} %shard_map.56), calls=%async_computation | async-start | bytes 131072 | tf_op jit(solution)/shard_map/all_to_all | solution.py:163
  11.3 10.9 %copy-start.2 = (s32[256,1]{0,1:T(1,128)S(1)}, s32[256,1]{0,1:T(1,128)}, u32[]{:S(2)}) copy-start(s32[256,1]{0,1:T(1,128)} %param.9) | copy-start | bytes 3076
  11.3 13.8 %collective-permute-start.1 = (bf16[16,1536]{1,0:T(8,128)(2,1)S(1)}, bf16[16,1536]{1,0:T(8,128)(2,1)S(1)}, u32[]{:S(2)}, u32[]{:S(2)}) collective-permute-start(bf16[16,1536]{1,0:T(8,128)(2,1)S(1)} %pad_maximum_fusion), channel_id=1, source_target_pairs={{0,31},{1,0},{2,1},{3,2},{4,3},{5,4},{6,5},{7,6},{8,7},{9,8},{10,9... | collective-permute-start | bytes 147464 | tf_op jit(solution)/shard_map/ppermute | solution.py:159
  22.3 0.7 %copy-start.3 = (s32[256,12]{0,1:T(8,128)S(1)}, s32[256,12]{0,1:T(8,128)}, u32[]{:S(2)}) copy-start(s32[256,12]{0,1:T(8,128)} %param.7) | copy-start | bytes 36868
  22.3 0.7 %copy-start.4 = (s32[256,12]{0,1:T(8,128)S(1)}, s32[256,12]{0,1:T(8,128)}, u32[]{:S(2)}) copy-start(s32[256,12]{0,1:T(8,128)} %param.8) | copy-start | bytes 36868
